TPU v7x, 512 devices: a whole 4x4x16 slice. The times are simulated.
512 devices in a mesh: dp: 32 (over z, x_hi), seq: 16 (over y, x_lo, core).
Axes of the slice: x: 4 (x_hi: 2, x_lo: 2; x = x_hi * 2 + x_lo), y: 4, z: 16, core: 2. Of those that a mesh axis runs over, the one named last changes fastest.
Arguments:
- attn_queries: bfloat16 [32, 2048, 4096], P('dp', 'seq'), may hold values from -5 to 5
- attention_key_rows: bfloat16 [32, 2048, 512], P('dp', 'seq'), may hold values from -5 to 5
- attention_value_rows: bfloat16 [32, 2048, 512], P('dp', 'seq'), may hold values from -6 to 6
- score_gain: float32 [32], replicated, may hold values from 0.6 to 1.4
- attn_grad: bfloat16 [32, 2048, 4096], P('dp', 'seq'), may hold values from -15 to 15
- segment_ids: int32 [32, 2048], P('dp'), may hold values from 0 to 31, never falling along the last dimension, each value on 1 to 256 neighbouring positions
Outputs:
- grad_queries: bfloat16 [32, 2048, 4096], P('dp', 'seq')
- key_gradient_rows: bfloat16 [32, 2048, 512], P('dp', 'seq')
- value_gradient_rows: bfloat16 [32, 2048, 512], P('dp', 'seq')
- grad_gain: float32 [32], P('seq')
Inputs may be any that keep to these rules, and one draw needn't show every extreme that they name: `segment_ids`: segment numbers never fall along a sequence; each document holds 1 to 256 positions, one exactly that many.
All inputs are finite; a program needn't handle non-finite values.
Results may differ from a plain program's by a relative error of at most 0.007.
Values may be sent and summed in bfloat16 or wider, within the bound.
A program may use at most 64 MiB of HBM per device.

v0:
```python
import functools
import math

import jax
import jax.numpy as jnp
from jax import lax
from jax.experimental import pallas as pl
from jax.experimental.pallas import tpu as pltpu
from jax.sharding import PartitionSpec as P

QUERY_HEADS = 32
KEY_VALUE_HEADS = 4
HEAD_SIZE = 128
GROUP = QUERY_HEADS // KEY_VALUE_HEADS
BLOCK = 128
HALF = 64
WINDOW = 320
QUAD = 4
LANES = QUAD * HALF
CHUNK = 64
LOG2E = math.log2(math.e)
SCALE = HEAD_SIZE ** -0.5
BF16 = jnp.bfloat16
F32 = jnp.float32
NT = (((1,), (1,)), ((), ()))
TN = (((0,), (0,)), ((), ()))


def fold_rows(x):
    return jnp.sum(x.reshape(x.shape[0] // 8, 8, x.shape[1]), axis=0)


def kernel(
    seq_size, dp_size, factor,
    q_hbm, k_hbm, v_hbm, gain_ref, g_hbm, seg_ref,
    dq_hbm, dk_hbm, dv_hbm, gain_out,
    qg, kv, ret_send, ret, acc, dq_buf, dkv_buf, seg_rows, bias,
    s_buf, dp_buf, y_buf, p_buf, ds_buf,
    g_part, g_in1, g_sum, g_in2,
    in_sem, own_sem, halo_send, halo_recv, back_send, back_recv, dq_sem, dkv_sem, gain_sem,
):
    me = lax.axis_index("seq")
    row = lax.axis_index("dp")

    def seq_at(offset):
        return lax.rem(me + offset, seq_size)

    def load(j, carry):
        wide = pl.ds(pl.multiple_of(j * (GROUP * HEAD_SIZE), GROUP * HEAD_SIZE), GROUP * HEAD_SIZE)
        thin = pl.ds(pl.multiple_of(j * HEAD_SIZE, HEAD_SIZE), HEAD_SIZE)
        pltpu.make_async_copy(k_hbm.at[:, thin], kv.at[j, 0, pl.ds(2 * BLOCK, BLOCK)], own_sem.at[j]).start()
        pltpu.make_async_copy(v_hbm.at[:, thin], kv.at[j, 1, pl.ds(2 * BLOCK, BLOCK)], own_sem.at[j]).start()
        pltpu.make_async_copy(q_hbm.at[:, wide], qg.at[j, 0], in_sem.at[j]).start()
        pltpu.make_async_copy(g_hbm.at[:, wide], qg.at[j, 1], in_sem.at[j]).start()
        return carry

    barrier = pltpu.get_barrier_semaphore()

    def greet_seq(i, carry):
        pl.semaphore_signal(barrier, inc=1, device_id={"seq": seq_at(i)}, device_id_type=pl.DeviceIdType.MESH)
        return carry

    def greet_dp(i, carry):
        pl.semaphore_signal(
            barrier, inc=1, device_id={"dp": lax.rem(row + i, dp_size)}, device_id_type=pl.DeviceIdType.MESH
        )
        return carry

    lax.fori_loop(1, seq_size, greet_seq, 0)
    lax.fori_loop(1, dp_size, greet_dp, 0)
    lax.fori_loop(0, KEY_VALUE_HEADS, load, 0)
    pl.semaphore_wait(barrier, seq_size + dp_size - 2)

    def halo_start(j):
        thin = pl.ds(pl.multiple_of(j * HEAD_SIZE, HEAD_SIZE), HEAD_SIZE)
        for which, source in enumerate((k_hbm, v_hbm)):
            for hop in (1, 2):
                pltpu.make_async_remote_copy(
                    src_ref=source.at[:, thin],
                    dst_ref=kv.at[j, which, pl.ds((2 - hop) * BLOCK, BLOCK)],
                    send_sem=halo_send.at[j],
                    recv_sem=halo_recv.at[j],
                    device_id={"seq": seq_at(hop)},
                    device_id_type=pl.DeviceIdType.MESH,
                ).start()

    halo_start(0)

    for b in range(3):
        place = pl.multiple_of(seq_at(seq_size - 2 + b) * BLOCK, BLOCK)
        ids = seg_ref[:, pl.ds(place, BLOCK)].astype(F32)
        seg_rows[pl.ds(b * BLOCK, BLOCK)] = jnp.transpose(jnp.broadcast_to(ids, (BLOCK, BLOCK)))
    own_ids = jnp.broadcast_to(
        seg_ref[:, pl.ds(pl.multiple_of(me * BLOCK, BLOCK), BLOCK)].astype(F32), (8, BLOCK)
    )
    turned = pltpu.roll(own_ids, HALF, 1)
    lane8 = lax.broadcasted_iota(jnp.int32, (8, BLOCK), 1)
    key_place = lax.broadcasted_iota(jnp.int32, (WINDOW, BLOCK), 0)
    lane = lax.broadcasted_iota(jnp.int32, (WINDOW, BLOCK), 1)
    for half in range(2):
        ids = jnp.where((lane8 < HALF) == (half == 0), own_ids, turned)[0:1]
        s_at = (me - 2) * BLOCK + half * HALF + key_place
        t_at = me * BLOCK + half * HALF + jnp.where(lane < HALF, lane, lane - HALF)
        allowed = (seg_rows[pl.ds(half * HALF, WINDOW)] == ids) & (s_at <= t_at) & (s_at >= 0)
        bias[half] = jnp.where(allowed, 0.0, -1e30)

    lane_wide = lax.broadcasted_iota(jnp.int32, (1, LANES), 1)

    def back_copy(j, hop):
        return pltpu.make_async_remote_copy(
            src_ref=ret_send.at[j, 2 - hop],
            dst_ref=ret.at[j, 2 - hop],
            send_sem=back_send.at[j],
            recv_sem=back_recv.at[j],
            device_id={"seq": seq_at(seq_size - hop)},
            device_id_type=pl.DeviceIdType.MESH,
        )

    def whole_back(j):
        return pltpu.make_async_remote_copy(
            src_ref=ret_send.at[j],
            dst_ref=ret.at[j],
            send_sem=back_send.at[j],
            recv_sem=back_recv.at[j],
            device_id={"seq": seq_at(1)},
            device_id_type=pl.DeviceIdType.MESH,
        )

    def dkv_out(j, which, target):
        thin = pl.ds(pl.multiple_of(j * HEAD_SIZE, HEAD_SIZE), HEAD_SIZE)
        return pltpu.make_async_copy(dkv_buf.at[j, which], target.at[:, thin], dkv_sem.at[j, which])

    def finish(j):
        whole_back(j).wait_recv()
        for which, target in enumerate((dk_hbm, dv_hbm)):
            total = (
                acc[j, which, pl.ds(2 * BLOCK, BLOCK)]
                + ret[j, 1, which].astype(F32)
                + ret[j, 0, which].astype(F32)
            )
            dkv_buf[j, which] = total.astype(BF16)
            dkv_out(j, which, target).start()

    def dq_out(j):
        wide = pl.ds(pl.multiple_of(j * (GROUP * HEAD_SIZE), GROUP * HEAD_SIZE), GROUP * HEAD_SIZE)
        return pltpu.make_async_copy(dq_buf.at[j], dq_hbm.at[:, wide], dq_sem.at[j])

    def gain_copy1(target):
        return pltpu.make_async_remote_copy(
            src_ref=g_part.at[target],
            dst_ref=g_in1.at[lax.rem(me - target + seq_size, seq_size) - 1],
            send_sem=gain_sem.at[0],
            recv_sem=gain_sem.at[1],
            device_id={"seq": target},
            device_id_type=pl.DeviceIdType.MESH,
        )

    units = [(half, quad) for half in range(2) for quad in range(GROUP // QUAD)]

    def group(j, carry):
        pltpu.make_async_remote_copy(
            src_ref=kv.at[j, :, pl.ds(0, 2 * BLOCK)],
            dst_ref=kv.at[j, :, pl.ds(0, 2 * BLOCK)],
            send_sem=halo_send.at[j],
            recv_sem=halo_recv.at[j],
            device_id={"seq": seq_at(1)},
            device_id_type=pl.DeviceIdType.MESH,
        ).wait_recv()

        @pl.when(j < KEY_VALUE_HEADS - 1)
        def _():
            halo_start(j + 1)

        own = kv.at[j, :, pl.ds(2 * BLOCK, BLOCK)]
        pltpu.make_async_copy(own, own, own_sem.at[j]).wait()
        pltpu.make_async_copy(qg.at[j], qg.at[j], in_sem.at[j]).wait()

        def stack(which, half, quad):
            return jnp.concatenate(
                [
                    qg[j, which, pl.ds(half * HALF, HALF), pl.ds((quad * QUAD + h) * HEAD_SIZE, HEAD_SIZE)]
                    for h in range(QUAD)
                ],
                axis=0,
            )

        def first(u):
            half, quad = units[u]
            rows = pl.ds(half * HALF, WINDOW)
            s_buf[u] = lax.dot_general(kv[j, 0, rows], stack(0, half, quad), NT, preferred_element_type=F32)
            dp_buf[u] = lax.dot_general(kv[j, 1, rows], stack(1, half, quad), NT, preferred_element_type=F32)

        def middle(u):
            half, quad = units[u]
            gains = [gain_ref[j * GROUP + quad * QUAD + h] for h in range(QUAD)]
            gain = jnp.where(
                lane_wide < 2 * HALF,
                jnp.where(lane_wide < HALF, gains[0], gains[1]),
                jnp.where(lane_wide < 3 * HALF, gains[2], gains[3]),
            )
            to_score = gain * (SCALE * LOG2E)
            to_grad = gain * SCALE
            chunks = [pl.ds(c, CHUNK) for c in range(0, WINDOW, CHUNK)]
            top = jnp.full((8, LANES), -3e38, F32)
            for rows in chunks:
                shade = bias[half, rows]
                y = s_buf[u, rows] * to_score + jnp.concatenate([shade, shade], axis=1)
                y_buf[u, rows] = y
                top = jnp.maximum(top, jnp.max(y.reshape(CHUNK // 8, 8, LANES), axis=0))
            top = jnp.max(top, axis=0, keepdims=True)
            total = jnp.zeros((8, LANES), F32)
            dot = jnp.zeros((8, LANES), F32)
            for rows in chunks:
                e = jnp.exp2(y_buf[u, rows] - top)
                y_buf[u, rows] = e
                total = total + fold_rows(e)
                dot = dot + fold_rows(e * dp_buf[u, rows])
            inverse = 1.0 / jnp.sum(total, axis=0, keepdims=True)
            delta = jnp.sum(dot, axis=0, keepdims=True) * inverse
            spread = jnp.zeros((8, LANES), F32)
            for rows in chunks:
                p = y_buf[u, rows] * inverse
                dscore = p * (dp_buf[u, rows] - delta)
                spread = spread + fold_rows(dscore * s_buf[u, rows])
                p_buf[u, rows] = p.astype(BF16)
                ds_buf[u, rows] = (dscore * to_grad).astype(BF16)
            return jnp.sum(spread, axis=0, keepdims=True) * (SCALE * factor)

        def last(u):
            half, quad = units[u]
            rows = pl.ds(half * HALF, WINDOW)
            ds = ds_buf[u]
            dk_new = jnp.dot(ds, stack(0, half, quad), preferred_element_type=F32)
            dv_new = jnp.dot(p_buf[u], stack(1, half, quad), preferred_element_type=F32)
            acc[j, 0, rows] += dk_new
            acc[j, 1, rows] += dv_new
            dq = lax.dot_general(ds, kv[j, 0, rows], TN, preferred_element_type=F32).astype(BF16)
            for h in range(QUAD):
                dq_buf[
                    j, pl.ds(half * HALF, HALF), pl.ds((quad * QUAD + h) * HEAD_SIZE, HEAD_SIZE)
                ] = dq[h * HALF:(h + 1) * HALF]

        acc[j] = jnp.zeros((2, 3 * BLOCK, HEAD_SIZE), F32)
        first(0)
        terms = []
        for u in range(len(units)):
            if u + 1 < len(units):
                first(u + 1)
            terms.append(middle(u))
            last(u)

        for place in range(2):
            for which in range(2):
                ret_send[j, place, which] = acc[j, which, pl.ds(place * BLOCK, BLOCK)].astype(BF16)
            back_copy(j, 2 - place).start()
        dq_out(j).start()

        per = GROUP // QUAD
        for quad in range(per):
            both = terms[quad] + terms[per + quad]
            for side in range(2):
                target = j * (GROUP // 2) + quad * 2 + side
                g_part[target] = both[:, side * 2 * HALF:(side + 1) * 2 * HALF]

                @pl.when(target != me)
                def _():
                    gain_copy1(target).start()

        @pl.when(j > 0)
        def _():
            finish(j - 1)

        return carry

    lax.fori_loop(0, KEY_VALUE_HEADS, group, 0)

    def whole_gain(buf, at):
        return pltpu.make_async_remote_copy(
            src_ref=buf,
            dst_ref=buf,
            send_sem=gain_sem.at[at],
            recv_sem=gain_sem.at[at + 1],
            device_id={"seq": seq_at(1)},
            device_id_type=pl.DeviceIdType.MESH,
        )

    whole_gain(g_in1, 0).wait_recv()
    g_sum[0] = g_part[me] + jnp.sum(g_in1[...], axis=0)

    def gain_send2(i, carry):
        pltpu.make_async_remote_copy(
            src_ref=g_sum.at[0],
            dst_ref=g_in2.at[i - 1],
            send_sem=gain_sem.at[2],
            recv_sem=gain_sem.at[3],
            device_id={"dp": lax.rem(row + i, dp_size)},
            device_id_type=pl.DeviceIdType.MESH,
        ).start()
        return carry

    lax.fori_loop(1, dp_size, gain_send2, 0)
    finish(KEY_VALUE_HEADS - 1)
    whole_gain(g_in2, 2).wait_recv()
    lanes = g_sum[0] + jnp.sum(g_in2[...], axis=0)
    lane1 = lax.broadcasted_iota(jnp.int32, (1, 2 * HALF), 1)
    low = jnp.sum(jnp.where(lane1 < HALF, lanes, 0.0), axis=1, keepdims=True)
    high = jnp.sum(jnp.where(lane1 < HALF, 0.0, lanes), axis=1, keepdims=True)
    gain_out[...] = jnp.where(lane1 == 0, low, high)

    whole_gain(g_in1, 0).wait_send()
    whole_gain(g_in2, 2).wait_send()

    def drain(j, carry):
        pltpu.make_async_remote_copy(
            src_ref=kv.at[j, :, pl.ds(0, 2 * BLOCK)],
            dst_ref=kv.at[j, :, pl.ds(0, 2 * BLOCK)],
            send_sem=halo_send.at[j],
            recv_sem=halo_recv.at[j],
            device_id={"seq": seq_at(1)},
            device_id_type=pl.DeviceIdType.MESH,
        ).wait_send()
        whole_back(j).wait_send()
        dq_out(j).wait()
        dkv_out(j, 0, dk_hbm).wait()
        dkv_out(j, 1, dv_hbm).wait()
        return carry

    lax.fori_loop(0, KEY_VALUE_HEADS, drain, 0)


def body(queries, keys, values, score_gain, grad, segment_ids):
    seq_size = lax.axis_size("seq")
    dp_size = lax.axis_size("dp")
    tokens = queries.shape[1]
    factor = 1.0 / (dp_size * tokens * seq_size)
    any_space = pl.BlockSpec(memory_space=pl.ANY)
    heads = KEY_VALUE_HEADS
    units = 2 * GROUP // QUAD
    wide = GROUP * HEAD_SIZE
    dq, dk, dv, gain = pl.pallas_call(
        functools.partial(kernel, seq_size, dp_size, factor),
        out_shape=(
            jax.ShapeDtypeStruct((BLOCK, QUERY_HEADS * HEAD_SIZE), BF16),
            jax.ShapeDtypeStruct((BLOCK, heads * HEAD_SIZE), BF16),
            jax.ShapeDtypeStruct((BLOCK, heads * HEAD_SIZE), BF16),
            jax.ShapeDtypeStruct((1, 2 * HALF), F32),
        ),
        in_specs=[
            any_space,
            any_space,
            any_space,
            pl.BlockSpec(memory_space=pltpu.SMEM),
            any_space,
            pl.BlockSpec(memory_space=pltpu.VMEM),
        ],
        out_specs=(any_space, any_space, any_space, pl.BlockSpec(memory_space=pltpu.VMEM)),
        scratch_shapes=[
            pltpu.VMEM((heads, 2, BLOCK, wide), BF16),
            pltpu.VMEM((heads, 2, 3 * BLOCK, HEAD_SIZE), BF16),
            pltpu.VMEM((heads, 2, 2, BLOCK, HEAD_SIZE), BF16),
            pltpu.VMEM((heads, 2, 2, BLOCK, HEAD_SIZE), BF16),
            pltpu.VMEM((heads, 2, 3 * BLOCK, HEAD_SIZE), F32),
            pltpu.VMEM((heads, BLOCK, wide), BF16),
            pltpu.VMEM((heads, 2, BLOCK, HEAD_SIZE), BF16),
            pltpu.VMEM((3 * BLOCK, BLOCK), F32),
            pltpu.VMEM((2, WINDOW, BLOCK), F32),
            pltpu.VMEM((units, WINDOW, LANES), F32),
            pltpu.VMEM((units, WINDOW, LANES), F32),
            pltpu.VMEM((units, WINDOW, LANES), F32),
            pltpu.VMEM((units, WINDOW, LANES), BF16),
            pltpu.VMEM((units, WINDOW, LANES), BF16),
            pltpu.VMEM((seq_size, 1, 2 * HALF), F32),
            pltpu.VMEM((seq_size - 1, 1, 2 * HALF), F32),
            pltpu.VMEM((1, 1, 2 * HALF), F32),
            pltpu.VMEM((dp_size - 1, 1, 2 * HALF), F32),
            pltpu.SemaphoreType.DMA((heads,)),
            pltpu.SemaphoreType.DMA((heads,)),
            pltpu.SemaphoreType.DMA((heads,)),
            pltpu.SemaphoreType.DMA((heads,)),
            pltpu.SemaphoreType.DMA((heads,)),
            pltpu.SemaphoreType.DMA((heads,)),
            pltpu.SemaphoreType.DMA((heads,)),
            pltpu.SemaphoreType.DMA((heads, 2)),
            pltpu.SemaphoreType.DMA((4,)),
        ],
        compiler_params=pltpu.CompilerParams(
            collective_id=0, has_side_effects=True, vmem_limit_bytes=48 * 1024 * 1024
        ),
        cost_estimate=pl.CostEstimate(
            flops=2 * 5 * BLOCK * WINDOW * HEAD_SIZE * QUERY_HEADS,
            bytes_accessed=4 * 1024 * 1024,
            transcendentals=BLOCK * WINDOW * QUERY_HEADS,
        ),
    )(queries[0], keys[0], values[0], score_gain, grad[0], segment_ids)
    return dq[None], dk[None], dv[None], gain[0, :2]


def solution(mesh):
    return jax.shard_map(
        body,
        mesh=mesh,
        in_specs=(
            P("dp", "seq", None),
            P("dp", "seq", None),
            P("dp", "seq", None),
            P(),
            P("dp", "seq", None),
            P("dp", None),
        ),
        out_specs=(P("dp", "seq", None), P("dp", "seq", None), P("dp", "seq", None), P("seq")),
        check_vma=False,
    )
```

profile of v0, /device:TPU:24, one launch (start us, length us, event | category | flops | bytes accessed | tf_op | source)
XLA Modules:
  0.0 57.9 jit_solution(6296612633710956814)
XLA Ops:
  0.6 0.0 copy-start.5
  0.6 0.6 %copy-done.5 = f32[32]{0:T(128)S(1)} copy-done((f32[32]{0:T(128)S(1)}, f32[32]{0:T(128)}, u32[]{:S(2)}) %copy-start.5) | copy-done | bytes 152
  1.3 0.0 copy-start
  1.3 1.2 %copy-done = bf16[1,128,4096]{2,1,0:T(8,128)(2,1)S(1)} copy-done((bf16[1,128,4096]{2,1,0:T(8,128)(2,1)S(1)}, bf16[1,128,4096]{2,1,0:T(8,128)(2,1)}, u32[]{:S(2)}) %copy-start) | copy-done | bytes 1048600
  2.5 0.0 copy-start.1
  2.5 1.2 %copy-done.1 = bf16[1,128,4096]{2,1,0:T(8,128)(2,1)S(1)} copy-done((bf16[1,128,4096]{2,1,0:T(8,128)(2,1)S(1)}, bf16[1,128,4096]{2,1,0:T(8,128)(2,1)}, u32[]{:S(2)}) %copy-start.1) | copy-done | bytes 1048600
  3.7 0.0 copy-start.2
  3.7 0.9 %copy-done.2 = bf16[1,128,512]{2,1,0:T(8,128)(2,1)S(1)} copy-done((bf16[1,128,512]{2,1,0:T(8,128)(2,1)S(1)}, bf16[1,128,512]{2,1,0:T(8,128)(2,1)}, u32[]{:S(2)}) %copy-start.2) | copy-done | bytes 131096
  4.6 0.0 copy-start.3
  4.6 0.9 %copy-done.3 = bf16[1,128,512]{2,1,0:T(8,128)(2,1)S(1)} copy-done((bf16[1,128,512]{2,1,0:T(8,128)(2,1)S(1)}, bf16[1,128,512]{2,1,0:T(8,128)(2,1)}, u32[]{:S(2)}) %copy-start.3) | copy-done | bytes 131096
  5.5 0.0 copy-start.4
  5.6 0.7 %copy-done.4 = s32[1,2048]{1,0:T(1,128)S(1)} copy-done((s32[1,2048]{1,0:T(1,128)S(1)}, s32[1,2048]{1,0:T(1,128)}, u32[]{:S(2)}) %copy-start.4) | copy-done | bytes 8216
  6.2 48.9 %shard_map.93 = (bf16[128,4096]{1,0:T(8,128)(2,1)S(1)}, bf16[128,512]{1,0:T(8,128)(2,1)S(1)}, bf16[128,512]{1,0:T(8,128)(2,1)S(1)}, f32[1,128]{1,0:T(1,128)S(1)}) custom-call(bf16[128,4096]{1,0:T(8,128)(2,1)S(1)} %bitcast.12, bf16[128,512]{1,0:T(8,128)(2,1)S(1)} %bitcast.14, bf16[128,512]{1,0:T(8,128)(2,1)S(1)} %bitcast.15, f32[32]{0:T(128)S(1)} %copy-done.5, ...), custom_call_target="tpu_custom_call" | custom-call | flops 1677721600 | bytes 4194304 | tf_op jit(solution)/shard_map/pallas_call | solution.py:340
  55.1 0.5 slice_bitcast_fusion
  55.7 1.0 %copy.13 = bf16[1,128,4096]{2,1,0:T(8,128)(2,1)} copy(bf16[1,128,4096]{2,1,0:T(8,128)(2,1)S(1)} %bitcast.9) | data formatting | bytes 2097152
  56.6 0.7 %copy.14 = bf16[1,128,512]{2,1,0:T(8,128)(2,1)} copy(bf16[1,128,512]{2,1,0:T(8,128)(2,1)S(1)} %bitcast.11) | data formatting | bytes 262144
  57.3 0.7 %copy.15 = bf16[1,128,512]{2,1,0:T(8,128)(2,1)} copy(bf16[1,128,512]{2,1,0:T(8,128)(2,1)S(1)} %bitcast.10) | data formatting | bytes 262144
Async XLA Ops:
  0.6 0.7 %copy-start.5 = (f32[32]{0:T(128)S(1)}, f32[32]{0:T(128)}, u32[]{:S(2)}) copy-start(f32[32]{0:T(128)} %gain_ref.1) | copy-start | bytes 388
  1.3 1.2 %copy-start = (bf16[1,128,4096]{2,1,0:T(8,128)(2,1)S(1)}, bf16[1,128,4096]{2,1,0:T(8,128)(2,1)}, u32[]{:S(2)}) copy-start(bf16[1,128,4096]{2,1,0:T(8,128)(2,1)} %param.6) | copy-start | bytes 3145732
  2.5 1.2 %copy-start.1 = (bf16[1,128,4096]{2,1,0:T(8,128)(2,1)S(1)}, bf16[1,128,4096]{2,1,0:T(8,128)(2,1)}, u32[]{:S(2)}) copy-start(bf16[1,128,4096]{2,1,0:T(8,128)(2,1)} %param.10) | copy-start | bytes 3145732
  3.7 0.9 %copy-start.2 = (bf16[1,128,512]{2,1,0:T(8,128)(2,1)S(1)}, bf16[1,128,512]{2,1,0:T(8,128)(2,1)}, u32[]{:S(2)}) copy-start(bf16[1,128,512]{2,1,0:T(8,128)(2,1)} %param.7) | copy-start | bytes 393220
  4.6 0.9 %copy-start.3 = (bf16[1,128,512]{2,1,0:T(8,128)(2,1)S(1)}, bf16[1,128,512]{2,1,0:T(8,128)(2,1)}, u32[]{:S(2)}) copy-start(bf16[1,128,512]{2,1,0:T(8,128)(2,1)} %param.8) | copy-start | bytes 393220
  5.5 0.7 %copy-start.4 = (s32[1,2048]{1,0:T(1,128)S(1)}, s32[1,2048]{1,0:T(1,128)}, u32[]{:S(2)}) copy-start(s32[1,2048]{1,0:T(1,128)} %seg_ref.1) | copy-start | bytes 24580
where the time goes:
time: 58.2 us; the launch traced here: 57.9 us
  Pallas kernels  48.9 us (84%)
  local copies, waits for them, and re-layouts  8.39 us (14%)
  between operations  0.66 us (1%)
    pallas_call x1, Pallas kernels, body(): pl.pallas_call(functools.partial(kernel, seq_size, dp_size, factor), out_...  48.9 us
    unnamed x15, local copies, waits for them, and re-layouts  7.88 us

commit v1 on v0

--- a/solution.py
+++ b/solution.py
@@ -18,6 +18,8 @@
 QUAD = 4
 LANES = QUAD * HALF
 CHUNK = 64
+HAND_PARTS = 4
+VMEM_BYTES = 64 * 1024 * 1024
 LOG2E = math.log2(math.e)
 SCALE = HEAD_SIZE ** -0.5
 BF16 = jnp.bfloat16
@@ -32,12 +34,12 @@
 
 def kernel(
     seq_size, dp_size, factor,
-    q_hbm, k_hbm, v_hbm, gain_ref, g_hbm, seg_ref,
+    q_hbm, k_hbm, v_hbm, gain_hbm, g_hbm, seg_hbm,
     dq_hbm, dk_hbm, dv_hbm, gain_out,
     qg, kv, ret_send, ret, acc, dq_buf, dkv_buf, seg_rows, bias,
-    s_buf, dp_buf, y_buf, p_buf, ds_buf,
+    s_buf, dp_buf, y_buf, p_buf, ds_buf, seg_ref, gain_ref,
     g_part, g_in1, g_sum, g_in2,
-    in_sem, own_sem, halo_send, halo_recv, back_send, back_recv, dq_sem, dkv_sem, gain_sem,
+    in_sem, own_sem, halo_send, halo_recv, back_send, back_recv, dq_sem, dkv_sem, gain_sem, small_sem,
 ):
     me = lax.axis_index("seq")
     row = lax.axis_index("dp")
@@ -68,6 +70,10 @@
 
     lax.fori_loop(1, seq_size, greet_seq, 0)
     lax.fori_loop(1, dp_size, greet_dp, 0)
+    seg_copy = pltpu.make_async_copy(seg_hbm, seg_ref, small_sem.at[0])
+    gain_copy = pltpu.make_async_copy(gain_hbm, gain_ref, small_sem.at[1])
+    seg_copy.start()
+    gain_copy.start()
     lax.fori_loop(0, KEY_VALUE_HEADS, load, 0)
     pl.semaphore_wait(barrier, seq_size + dp_size - 2)
 
@@ -84,7 +90,19 @@
                     device_id_type=pl.DeviceIdType.MESH,
                 ).start()
 
+    def halo_whole(j):
+        return pltpu.make_async_remote_copy(
+            src_ref=kv.at[j, :, pl.ds(0, 2 * BLOCK)],
+            dst_ref=kv.at[j, :, pl.ds(0, 2 * BLOCK)],
+            send_sem=halo_send.at[j],
+            recv_sem=halo_recv.at[j],
+            device_id={"seq": seq_at(1)},
+            device_id_type=pl.DeviceIdType.MESH,
+        )
+
     halo_start(0)
+    seg_copy.wait()
+    gain_copy.wait()
 
     for b in range(3):
         place = pl.multiple_of(seq_at(seq_size - 2 + b) * BLOCK, BLOCK)
@@ -155,17 +173,10 @@
             device_id_type=pl.DeviceIdType.MESH,
         )
 
-    units = [(half, quad) for half in range(2) for quad in range(GROUP // QUAD)]
+    quads = GROUP // QUAD
 
     def group(j, carry):
-        pltpu.make_async_remote_copy(
-            src_ref=kv.at[j, :, pl.ds(0, 2 * BLOCK)],
-            dst_ref=kv.at[j, :, pl.ds(0, 2 * BLOCK)],
-            send_sem=halo_send.at[j],
-            recv_sem=halo_recv.at[j],
-            device_id={"seq": seq_at(1)},
-            device_id_type=pl.DeviceIdType.MESH,
-        ).wait_recv()
+        halo_whole(j).wait_recv()
 
         @pl.when(j < KEY_VALUE_HEADS - 1)
         def _():
@@ -175,23 +186,26 @@
         pltpu.make_async_copy(own, own, own_sem.at[j]).wait()
         pltpu.make_async_copy(qg.at[j], qg.at[j], in_sem.at[j]).wait()
 
-        def stack(which, half, quad):
+        def stack(which, half, heads):
             return jnp.concatenate(
                 [
-                    qg[j, which, pl.ds(half * HALF, HALF), pl.ds((quad * QUAD + h) * HEAD_SIZE, HEAD_SIZE)]
-                    for h in range(QUAD)
+                    qg[j, which, pl.ds(half * HALF, HALF), pl.ds(h * HEAD_SIZE, HEAD_SIZE)]
+                    for h in heads
                 ],
                 axis=0,
             )
 
-        def first(u):
-            half, quad = units[u]
+        def first(half, quad):
             rows = pl.ds(half * HALF, WINDOW)
-            s_buf[u] = lax.dot_general(kv[j, 0, rows], stack(0, half, quad), NT, preferred_element_type=F32)
-            dp_buf[u] = lax.dot_general(kv[j, 1, rows], stack(1, half, quad), NT, preferred_element_type=F32)
-
-        def middle(u):
-            half, quad = units[u]
+            heads = range(quad * QUAD, quad * QUAD + QUAD)
+            s_buf[half, quad] = lax.dot_general(
+                kv[j, 0, rows], stack(0, half, heads), NT, preferred_element_type=F32
+            )
+            dp_buf[half, quad] = lax.dot_general(
+                kv[j, 1, rows], stack(1, half, heads), NT, preferred_element_type=F32
+            )
+
+        def middle(half, quad):
             gains = [gain_ref[j * GROUP + quad * QUAD + h] for h in range(QUAD)]
             gain = jnp.where(
                 lane_wide < 2 * HALF,
@@ -200,54 +214,66 @@
             )
             to_score = gain * (SCALE * LOG2E)
             to_grad = gain * SCALE
+            lanes = pl.ds(quad * LANES, LANES)
             chunks = [pl.ds(c, CHUNK) for c in range(0, WINDOW, CHUNK)]
             top = jnp.full((8, LANES), -3e38, F32)
             for rows in chunks:
                 shade = bias[half, rows]
-                y = s_buf[u, rows] * to_score + jnp.concatenate([shade, shade], axis=1)
-                y_buf[u, rows] = y
+                y = s_buf[half, quad, rows] * to_score + jnp.concatenate([shade, shade], axis=1)
+                y_buf[half, quad, rows] = y
                 top = jnp.maximum(top, jnp.max(y.reshape(CHUNK // 8, 8, LANES), axis=0))
             top = jnp.max(top, axis=0, keepdims=True)
             total = jnp.zeros((8, LANES), F32)
             dot = jnp.zeros((8, LANES), F32)
             for rows in chunks:
-                e = jnp.exp2(y_buf[u, rows] - top)
-                y_buf[u, rows] = e
+                e = jnp.exp2(y_buf[half, quad, rows] - top)
+                y_buf[half, quad, rows] = e
                 total = total + fold_rows(e)
-                dot = dot + fold_rows(e * dp_buf[u, rows])
+                dot = dot + fold_rows(e * dp_buf[half, quad, rows])
             inverse = 1.0 / jnp.sum(total, axis=0, keepdims=True)
             delta = jnp.sum(dot, axis=0, keepdims=True) * inverse
             spread = jnp.zeros((8, LANES), F32)
             for rows in chunks:
-                p = y_buf[u, rows] * inverse
-                dscore = p * (dp_buf[u, rows] - delta)
-                spread = spread + fold_rows(dscore * s_buf[u, rows])
-                p_buf[u, rows] = p.astype(BF16)
-                ds_buf[u, rows] = (dscore * to_grad).astype(BF16)
+                p = y_buf[half, quad, rows] * inverse
+                dscore = p * (dp_buf[half, quad, rows] - delta)
+                spread = spread + fold_rows(dscore * s_buf[half, quad, rows])
+                p_buf[half, rows, lanes] = p.astype(BF16)
+                ds_buf[half, rows, lanes] = (dscore * to_grad).astype(BF16)
             return jnp.sum(spread, axis=0, keepdims=True) * (SCALE * factor)
 
-        def last(u):
-            half, quad = units[u]
+        def last(half):
             rows = pl.ds(half * HALF, WINDOW)
-            ds = ds_buf[u]
-            dk_new = jnp.dot(ds, stack(0, half, quad), preferred_element_type=F32)
-            dv_new = jnp.dot(p_buf[u], stack(1, half, quad), preferred_element_type=F32)
-            acc[j, 0, rows] += dk_new
-            acc[j, 1, rows] += dv_new
-            dq = lax.dot_general(ds, kv[j, 0, rows], TN, preferred_element_type=F32).astype(BF16)
-            for h in range(QUAD):
-                dq_buf[
-                    j, pl.ds(half * HALF, HALF), pl.ds((quad * QUAD + h) * HEAD_SIZE, HEAD_SIZE)
-                ] = dq[h * HALF:(h + 1) * HALF]
-
-        acc[j] = jnp.zeros((2, 3 * BLOCK, HEAD_SIZE), F32)
-        first(0)
-        terms = []
-        for u in range(len(units)):
-            if u + 1 < len(units):
-                first(u + 1)
-            terms.append(middle(u))
-            last(u)
+            everyone = range(GROUP)
+            turned_keys = jnp.transpose(kv[j, 0, rows])
+            for quad in range(quads):
+                ds = ds_buf[half, :, pl.ds(quad * LANES, LANES)]
+                dq = jnp.dot(turned_keys, ds, preferred_element_type=F32).astype(BF16)
+                dq = jnp.transpose(dq)
+                for h in range(QUAD):
+                    dq_buf[
+                        j, pl.ds(half * HALF, HALF), pl.ds((quad * QUAD + h) * HEAD_SIZE, HEAD_SIZE)
+                    ] = dq[h * HALF:(h + 1) * HALF]
+            dk_new = jnp.dot(ds_buf[half], stack(0, half, everyone), preferred_element_type=F32)
+            dv_new = jnp.dot(p_buf[half], stack(1, half, everyone), preferred_element_type=F32)
+            if half == 0:
+                acc[j, 0, rows] = dk_new
+                acc[j, 1, rows] = dv_new
+                acc[j, :, pl.ds(WINDOW, HALF)] = jnp.zeros((2, HALF, HEAD_SIZE), F32)
+            else:
+                acc[j, 0, rows] += dk_new
+                acc[j, 1, rows] += dv_new
+
+        first(0, 0)
+        first(0, 1)
+        term00 = middle(0, 0)
+        first(1, 0)
+        term01 = middle(0, 1)
+        first(1, 1)
+        last(0)
+        term10 = middle(1, 0)
+        term11 = middle(1, 1)
+        last(1)
+        terms = [term00 + term10, term01 + term11]
 
         for place in range(2):
             for which in range(2):
@@ -255,9 +281,8 @@
             back_copy(j, 2 - place).start()
         dq_out(j).start()
 
-        per = GROUP // QUAD
-        for quad in range(per):
-            both = terms[quad] + terms[per + quad]
+        for quad in range(quads):
+            both = terms[quad]
             for side in range(2):
                 target = j * (GROUP // 2) + quad * 2 + side
                 g_part[target] = both[:, side * 2 * HALF:(side + 1) * 2 * HALF]
@@ -303,22 +328,14 @@
     whole_gain(g_in2, 2).wait_recv()
     lanes = g_sum[0] + jnp.sum(g_in2[...], axis=0)
     lane1 = lax.broadcasted_iota(jnp.int32, (1, 2 * HALF), 1)
-    low = jnp.sum(jnp.where(lane1 < HALF, lanes, 0.0), axis=1, keepdims=True)
-    high = jnp.sum(jnp.where(lane1 < HALF, 0.0, lanes), axis=1, keepdims=True)
-    gain_out[...] = jnp.where(lane1 == 0, low, high)
+    gain_out[0] = jnp.sum(jnp.where(lane1 < HALF, lanes, 0.0))
+    gain_out[1] = jnp.sum(jnp.where(lane1 < HALF, 0.0, lanes))
 
     whole_gain(g_in1, 0).wait_send()
     whole_gain(g_in2, 2).wait_send()
 
     def drain(j, carry):
-        pltpu.make_async_remote_copy(
-            src_ref=kv.at[j, :, pl.ds(0, 2 * BLOCK)],
-            dst_ref=kv.at[j, :, pl.ds(0, 2 * BLOCK)],
-            send_sem=halo_send.at[j],
-            recv_sem=halo_recv.at[j],
-            device_id={"seq": seq_at(1)},
-            device_id_type=pl.DeviceIdType.MESH,
-        ).wait_send()
+        halo_whole(j).wait_send()
         whole_back(j).wait_send()
         dq_out(j).wait()
         dkv_out(j, 0, dk_hbm).wait()
@@ -326,6 +343,21 @@
         return carry
 
     lax.fori_loop(0, KEY_VALUE_HEADS, drain, 0)
+
+
+def hand_over(dq_in, dk_in, dv_in, gain_in, dq_out, dk_out, dv_out, gain_to, sems):
+    copies = [
+        pltpu.make_async_copy(dk_in, dk_out, sems.at[HAND_PARTS]),
+        pltpu.make_async_copy(dv_in, dv_out, sems.at[HAND_PARTS + 1]),
+        pltpu.make_async_copy(gain_in, gain_to, sems.at[HAND_PARTS + 2]),
+    ]
+    for i in range(HAND_PARTS):
+        rows = pl.ds(i * (BLOCK // HAND_PARTS), BLOCK // HAND_PARTS)
+        copies.append(pltpu.make_async_copy(dq_in.at[rows], dq_out.at[rows], sems.at[i]))
+    for copy in copies:
+        copy.start()
+    for copy in copies:
+        copy.wait()
 
 
 def body(queries, keys, values, score_gain, grad, segment_ids):
@@ -333,9 +365,9 @@
     dp_size = lax.axis_size("dp")
     tokens = queries.shape[1]
     factor = 1.0 / (dp_size * tokens * seq_size)
-    any_space = pl.BlockSpec(memory_space=pl.ANY)
+    hbm = pl.BlockSpec(memory_space=pltpu.HBM)
     heads = KEY_VALUE_HEADS
-    units = 2 * GROUP // QUAD
+    quads = GROUP // QUAD
     wide = GROUP * HEAD_SIZE
     dq, dk, dv, gain = pl.pallas_call(
         functools.partial(kernel, seq_size, dp_size, factor),
@@ -343,17 +375,10 @@
             jax.ShapeDtypeStruct((BLOCK, QUERY_HEADS * HEAD_SIZE), BF16),
             jax.ShapeDtypeStruct((BLOCK, heads * HEAD_SIZE), BF16),
             jax.ShapeDtypeStruct((BLOCK, heads * HEAD_SIZE), BF16),
-            jax.ShapeDtypeStruct((1, 2 * HALF), F32),
+            jax.ShapeDtypeStruct((2,), F32),
         ),
-        in_specs=[
-            any_space,
-            any_space,
-            any_space,
-            pl.BlockSpec(memory_space=pltpu.SMEM),
-            any_space,
-            pl.BlockSpec(memory_space=pltpu.VMEM),
-        ],
-        out_specs=(any_space, any_space, any_space, pl.BlockSpec(memory_space=pltpu.VMEM)),
+        in_specs=[hbm] * 6,
+        out_specs=(hbm, hbm, hbm, pl.BlockSpec(memory_space=pltpu.SMEM)),
         scratch_shapes=[
             pltpu.VMEM((heads, 2, BLOCK, wide), BF16),
             pltpu.VMEM((heads, 2, 3 * BLOCK, HEAD_SIZE), BF16),
@@ -364,11 +389,13 @@
             pltpu.VMEM((heads, 2, BLOCK, HEAD_SIZE), BF16),
             pltpu.VMEM((3 * BLOCK, BLOCK), F32),
             pltpu.VMEM((2, WINDOW, BLOCK), F32),
-            pltpu.VMEM((units, WINDOW, LANES), F32),
-            pltpu.VMEM((units, WINDOW, LANES), F32),
-            pltpu.VMEM((units, WINDOW, LANES), F32),
-            pltpu.VMEM((units, WINDOW, LANES), BF16),
-            pltpu.VMEM((units, WINDOW, LANES), BF16),
+            pltpu.VMEM((2, quads, WINDOW, LANES), F32),
+            pltpu.VMEM((2, quads, WINDOW, LANES), F32),
+            pltpu.VMEM((2, quads, WINDOW, LANES), F32),
+            pltpu.VMEM((2, WINDOW, quads * LANES), BF16),
+            pltpu.VMEM((2, WINDOW, quads * LANES), BF16),
+            pltpu.VMEM((1, tokens * seq_size), jnp.int32),
+            pltpu.SMEM((QUERY_HEADS,), F32),
             pltpu.VMEM((seq_size, 1, 2 * HALF), F32),
             pltpu.VMEM((seq_size - 1, 1, 2 * HALF), F32),
             pltpu.VMEM((1, 1, 2 * HALF), F32),
@@ -382,9 +409,10 @@
             pltpu.SemaphoreType.DMA((heads,)),
             pltpu.SemaphoreType.DMA((heads, 2)),
             pltpu.SemaphoreType.DMA((4,)),
+            pltpu.SemaphoreType.DMA((2,)),
         ],
         compiler_params=pltpu.CompilerParams(
-            collective_id=0, has_side_effects=True, vmem_limit_bytes=48 * 1024 * 1024
+            collective_id=0, has_side_effects=True, vmem_limit_bytes=VMEM_BYTES
         ),
         cost_estimate=pl.CostEstimate(
             flops=2 * 5 * BLOCK * WINDOW * HEAD_SIZE * QUERY_HEADS,
@@ -392,7 +420,16 @@
             transcendentals=BLOCK * WINDOW * QUERY_HEADS,
         ),
     )(queries[0], keys[0], values[0], score_gain, grad[0], segment_ids)
-    return dq[None], dk[None], dv[None], gain[0, :2]
+    results = (dq, dk, dv, gain)
+    dq, dk, dv, gain = pl.pallas_call(
+        hand_over,
+        out_shape=tuple(jax.ShapeDtypeStruct(x.shape, x.dtype) for x in results),
+        in_specs=[hbm] * 4,
+        out_specs=(hbm,) * 4,
+        scratch_shapes=[pltpu.SemaphoreType.DMA((HAND_PARTS + 3,))],
+        compiler_params=pltpu.CompilerParams(vmem_limit_bytes=VMEM_BYTES),
+    )(*results)
+    return dq[None], dk[None], dv[None], gain
 
 
 def solution(mesh):

time: 58.2 us -> 91.3 us (1.57)
  Pallas kernels: 48.9 us -> 90.6 us
  local copies, waits for them, and re-layouts: 8.39 us -> 0 us
    pallas_call x0 -> x1, Pallas kernels: none -> 40.9 us  [body(): pl.pallas_call(hand_over, out_shape=tuple((jax.ShapeDtypeStruct(x.shape,...]
    unnamed x15 -> x0, local copies, waits for them, and re-layouts: 7.88 us -> none
where the time goes in v1:
time: 91.3 us; the launch traced here: 91.2 us
  Pallas kernels  90.6 us (99%)
    pallas_call x1, Pallas kernels, body(): pl.pallas_call(functools.partial(kernel, seq_size, dp_size, factor), out_...  49.7 us
    pallas_call x1, Pallas kernels, body(): pl.pallas_call(hand_over, out_shape=tuple((jax.ShapeDtypeStruct(x.shape,...  40.9 us

profile of v1, /device:TPU:24, one launch (start us, length us, event | category | flops | bytes accessed | tf_op | source)
XLA Modules:
  0.0 91.2 jit_solution(10749238142157169474)
XLA Ops:
  0.6 49.7 %shard_map.93 = (bf16[128,4096]{1,0:T(8,128)(2,1)}, bf16[128,512]{1,0:T(8,128)(2,1)}, bf16[128,512]{1,0:T(8,128)(2,1)}, f32[2]{0:T(128)}) custom-call(bf16[128,4096]{1,0:T(8,128)(2,1)} %bitcast.7, bf16[128,512]{1,0:T(8,128)(2,1)} %bitcast.10, bf16[128,512]{1,0:T(8,128)(2,1)} %bitcast.11, f32[32]{0:T(128)} %gain_hbm.1, bf16[128,4096]{1,0:T(8,128)(2,1)} %bitcast.8, ...), custom_call_target="tpu_custom_call" | custom-call | flops 1677721600 | bytes 4194304 | tf_op jit(solution)/shard_map/pallas_call | solution.py:372
  50.3 40.9 %shard_map.94 = (bf16[128,4096]{1,0:T(8,128)(2,1)}, bf16[128,512]{1,0:T(8,128)(2,1)}, bf16[128,512]{1,0:T(8,128)(2,1)}, f32[2]{0:T(128)}) custom-call(bf16[128,4096]{1,0:T(8,128)(2,1)} %get-tuple-element.12.dq_in, bf16[128,512]{1,0:T(8,128)(2,1)} %get-tuple-element.13.dk_in, bf16[128,512]{1,0:T(8,128)(2,1)} %get-tuple-element.14.dv_in, ...), custom_call_target="tpu_custom_call" | custom-call | tf_op jit(solution)/shard_map/pallas_call | solution.py:424

commit v2 on v1

v2 whole, which is shorter than its diff:
```python
import functools
import math

import jax
import jax.numpy as jnp
from jax import lax
from jax.experimental import pallas as pl
from jax.experimental.pallas import tpu as pltpu
from jax.sharding import PartitionSpec as P

QUERY_HEADS = 32
KEY_VALUE_HEADS = 4
HEAD_SIZE = 128
GROUP = QUERY_HEADS // KEY_VALUE_HEADS
BLOCK = 128
HALF = 64
WINDOW = 320
QUAD = 4
LANES = QUAD * HALF
CHUNK = 64
HAND_PARTS = 4
VMEM_BYTES = 64 * 1024 * 1024
LOG2E = math.log2(math.e)
SCALE = HEAD_SIZE ** -0.5
BF16 = jnp.bfloat16
F32 = jnp.float32
NT = (((1,), (1,)), ((), ()))
TN = (((0,), (0,)), ((), ()))


def fold_rows(x):
    return jnp.sum(x.reshape(x.shape[0] // 8, 8, x.shape[1]), axis=0)


def kernel(
    seq_size, dp_size, factor,
    q_hbm, k_hbm, v_hbm, gain_hbm, g_hbm, seg_hbm,
    dq_hbm, dk_hbm, dv_hbm, gain_out,
    qg, kv, ret_send, ret, mate_send, mate_in, acc, dq_buf, dkv_buf, seg_rows, bias,
    s_buf, dp_buf, y_buf, p_buf, ds_buf, seg_ref, gain_ref,
    g_rows, g_part, g_in1, g_sum, g_in2,
    in_sem, own_sem, halo_send, halo_recv, mate_kv_send, mate_kv_recv, mate_qg_send, mate_qg_recv,
    back_send, back_recv, mate_back_send, mate_back_recv, dq_sem, mate_dq_send, mate_dq_recv,
    dkv_sem, gain1_send, gain1_recv, gain2_sem, small_sem,
):
    me = lax.axis_index("seq")
    row = lax.axis_index("dp")
    chips = seq_size // 2
    chip = lax.div(me, 2)
    core = me - 2 * chip
    other = 1 - core
    mate = 2 * chip + other
    next_chip = lax.rem(chip + 1, chips)
    last_chip = lax.rem(chip + chips - 1, chips)

    def thin(head):
        return pl.ds(pl.multiple_of(head * HEAD_SIZE, HEAD_SIZE), HEAD_SIZE)

    def wide(head):
        return pl.ds(pl.multiple_of(head * (GROUP * HEAD_SIZE), GROUP * HEAD_SIZE), GROUP * HEAD_SIZE)

    def block(index):
        return pl.ds(pl.multiple_of(index * BLOCK, BLOCK), BLOCK)

    def remote(source, target, send, recv, device):
        return pltpu.make_async_remote_copy(
            src_ref=source,
            dst_ref=target,
            send_sem=send,
            recv_sem=recv,
            device_id={"seq": device},
            device_id_type=pl.DeviceIdType.MESH,
        )

    barrier = pltpu.get_barrier_semaphore()

    def greet_seq(i, carry):
        pl.semaphore_signal(
            barrier, inc=1, device_id={"seq": lax.rem(me + i, seq_size)}, device_id_type=pl.DeviceIdType.MESH
        )
        return carry

    def greet_dp(i, carry):
        pl.semaphore_signal(
            barrier, inc=1, device_id={"dp": lax.rem(row + i, dp_size)}, device_id_type=pl.DeviceIdType.MESH
        )
        return carry

    lax.fori_loop(1, seq_size, greet_seq, 0)
    lax.fori_loop(1, dp_size, greet_dp, 0)

    for a in range(2):
        head = 2 * core + a
        pltpu.make_async_copy(k_hbm.at[:, thin(head)], kv.at[a, 0, block(2 + core)], own_sem.at[a]).start()
        pltpu.make_async_copy(v_hbm.at[:, thin(head)], kv.at[a, 1, block(2 + core)], own_sem.at[a]).start()
        pltpu.make_async_copy(q_hbm.at[:, wide(head)], qg.at[a, 0, block(core)], in_sem.at[a]).start()
        pltpu.make_async_copy(g_hbm.at[:, wide(head)], qg.at[a, 1, block(core)], in_sem.at[a]).start()
    seg_copy = pltpu.make_async_copy(seg_hbm, seg_ref, small_sem.at[0])
    gain_copy = pltpu.make_async_copy(gain_hbm, gain_ref, small_sem.at[1])
    seg_copy.start()
    gain_copy.start()
    pl.semaphore_wait(barrier, seq_size + dp_size - 2)

    def halo_start(a):
        for to_core in range(2):
            for which, source in enumerate((k_hbm, v_hbm)):
                remote(
                    source.at[:, thin(2 * to_core + a)],
                    kv.at[a, which, block(core)],
                    halo_send.at[a],
                    halo_recv.at[a],
                    2 * next_chip + to_core,
                ).start()

    def halo_whole(a):
        part = kv.at[a, :, pl.ds(0, 2 * BLOCK)]
        return remote(part, part, halo_send.at[a], halo_recv.at[a], 2 * next_chip)

    def mate_start(a):
        head = 2 * other + a
        for which, source in enumerate((k_hbm, v_hbm)):
            remote(
                source.at[:, thin(head)], kv.at[a, which, block(2 + core)],
                mate_kv_send.at[a], mate_kv_recv.at[a], mate,
            ).start()
        for which, source in enumerate((q_hbm, g_hbm)):
            remote(
                source.at[:, wide(head)], qg.at[a, which, block(core)],
                mate_qg_send.at[a], mate_qg_recv.at[a], mate,
            ).start()

    def mate_kv(a):
        part = kv.at[a, :, block(2 + other)]
        return remote(part, part, mate_kv_send.at[a], mate_kv_recv.at[a], mate)

    def mate_qg(a):
        part = qg.at[a, :, block(other)]
        return remote(part, part, mate_qg_send.at[a], mate_qg_recv.at[a], mate)

    halo_start(0)
    mate_start(0)
    mate_start(1)
    seg_copy.wait()
    gain_copy.wait()

    def ids_of(index):
        place = pl.multiple_of(lax.rem(2 * chip + index + seq_size, seq_size) * BLOCK, BLOCK)
        return seg_ref[:, pl.ds(place, BLOCK)].astype(F32)

    for b in range(4):
        seg_rows[pl.ds(b * BLOCK, BLOCK)] = jnp.transpose(
            jnp.broadcast_to(ids_of(b - 2), (BLOCK, BLOCK))
        )
    lane8 = lax.broadcasted_iota(jnp.int32, (8, BLOCK), 1)
    key_place = lax.broadcasted_iota(jnp.int32, (WINDOW, BLOCK), 0)
    lane = lax.broadcasted_iota(jnp.int32, (WINDOW, BLOCK), 1)
    causal = key_place <= 2 * BLOCK + jnp.where(lane < HALF, lane, lane - HALF)
    for x in range(2):
        query_ids = jnp.broadcast_to(ids_of(x), (8, BLOCK))
        turned = pltpu.roll(query_ids, HALF, 1)
        for half in range(2):
            start = x * BLOCK + half * HALF
            ids = jnp.where((lane8 < HALF) == (half == 0), query_ids, turned)[0:1]
            inside = (chip - 1) * (2 * BLOCK) + start + key_place >= 0
            allowed = (seg_rows[pl.ds(start, WINDOW)] == ids) & causal & inside
            bias[2 * x + half] = jnp.where(allowed, 0.0, -1e30)

    lane_wide = lax.broadcasted_iota(jnp.int32, (1, LANES), 1)
    quads = GROUP // QUAD

    def back_copy(a, place):
        return remote(
            ret_send.at[a, place], ret.at[2 * core + a],
            back_send.at[a], back_recv.at[2 * core + a], 2 * last_chip + place,
        )

    def back_whole(a):
        return remote(ret_send.at[a], ret_send.at[a], back_send.at[a], back_recv.at[a], 2 * last_chip)

    def back_from(head):
        return remote(ret.at[head], ret.at[head], back_send.at[0], back_recv.at[head], 2 * last_chip)

    def mate_back(a):
        return remote(
            mate_send.at[a], mate_in.at[a], mate_back_send.at[a], mate_back_recv.at[a], mate
        )

    def dkv_out(head, which):
        target = (dk_hbm, dv_hbm)[which]
        return pltpu.make_async_copy(
            dkv_buf.at[head, which], target.at[:, thin(head)], dkv_sem.at[head, which]
        )

    def finish(a):
        mine = 2 * core + a
        theirs = 2 * other + a
        back_from(mine).wait_recv()
        for which in range(2):
            total = acc[a, which, block(2 + core)] + ret[mine, which].astype(F32)
            dkv_buf[mine, which] = total.astype(BF16)
            dkv_out(mine, which).start()
        mate_back(a).wait_recv()
        back_from(theirs).wait_recv()
        for which in range(2):
            total = mate_in[a, which].astype(F32) + ret[theirs, which].astype(F32)
            dkv_buf[theirs, which] = total.astype(BF16)
            dkv_out(theirs, which).start()

    def dq_own(a):
        return pltpu.make_async_copy(dq_buf.at[a, 0], dq_hbm.at[:, wide(2 * core + a)], dq_sem.at[a])

    def dq_mate(a):
        return remote(
            dq_buf.at[a, 1], dq_hbm.at[:, wide(2 * core + a)], mate_dq_send.at[a], mate_dq_recv.at[a], mate
        )

    def dq_from(a):
        part = dq_hbm.at[:, wide(2 * other + a)]
        return remote(part, part, mate_dq_send.at[a], mate_dq_recv.at[a], mate)

    def gain_copy1(index):
        return remote(
            g_part.at[index], g_in1.at[chip], gain1_send.at[index], gain1_recv.at[chip], chips * core + index
        )

    def step(number, carry):
        a = lax.div(number, 2)
        late = number - 2 * a
        x = core + late - 2 * core * late
        base = x * BLOCK

        @pl.when(late == 0)
        def _():
            halo_whole(a).wait_recv()

            @pl.when(a == 0)
            def _():
                halo_start(1)

            own = kv.at[a, :, block(2 + core)]
            pltpu.make_async_copy(own, own, own_sem.at[a]).wait()
            held = qg.at[a, :, block(core)]
            pltpu.make_async_copy(held, held, in_sem.at[a]).wait()
            mate_kv(a).wait_recv()
            acc[a] = jnp.zeros((2, 4 * BLOCK, HEAD_SIZE), F32)

        @pl.when(late == 1)
        def _():
            mate_qg(a).wait_recv()

        def key_rows(half):
            return pl.ds(pl.multiple_of(base + half * HALF, HALF), WINDOW)

        def stack(which, half, heads):
            rows = pl.ds(pl.multiple_of(base + half * HALF, HALF), HALF)
            return jnp.concatenate(
                [qg[a, which, rows, pl.ds(h * HEAD_SIZE, HEAD_SIZE)] for h in heads], axis=0
            )

        def first(half, quad):
            rows = key_rows(half)
            heads = range(quad * QUAD, quad * QUAD + QUAD)
            s_buf[half, quad] = lax.dot_general(
                kv[a, 0, rows], stack(0, half, heads), NT, preferred_element_type=F32
            )
            dp_buf[half, quad] = lax.dot_general(
                kv[a, 1, rows], stack(1, half, heads), NT, preferred_element_type=F32
            )

        def middle(half, quad):
            gains = [gain_ref[(2 * core + a) * GROUP + quad * QUAD + h] for h in range(QUAD)]
            gain = jnp.where(
                lane_wide < 2 * HALF,
                jnp.where(lane_wide < HALF, gains[0], gains[1]),
                jnp.where(lane_wide < 3 * HALF, gains[2], gains[3]),
            )
            to_score = gain * (SCALE * LOG2E)
            to_grad = gain * SCALE
            lanes = pl.ds(quad * LANES, LANES)
            chunks = [pl.ds(i, CHUNK) for i in range(0, WINDOW, CHUNK)]
            top = jnp.full((8, LANES), -3e38, F32)
            for rows in chunks:
                shade = bias[2 * x + half, rows]
                y = s_buf[half, quad, rows] * to_score + jnp.concatenate([shade, shade], axis=1)
                y_buf[half, quad, rows] = y
                top = jnp.maximum(top, jnp.max(y.reshape(CHUNK // 8, 8, LANES), axis=0))
            top = jnp.max(top, axis=0, keepdims=True)
            total = jnp.zeros((8, LANES), F32)
            dot = jnp.zeros((8, LANES), F32)
            for rows in chunks:
                e = jnp.exp2(y_buf[half, quad, rows] - top)
                y_buf[half, quad, rows] = e
                total = total + fold_rows(e)
                dot = dot + fold_rows(e * dp_buf[half, quad, rows])
            inverse = 1.0 / jnp.sum(total, axis=0, keepdims=True)
            delta = jnp.sum(dot, axis=0, keepdims=True) * inverse
            spread = jnp.zeros((8, LANES), F32)
            for rows in chunks:
                p = y_buf[half, quad, rows] * inverse
                dscore = p * (dp_buf[half, quad, rows] - delta)
                spread = spread + fold_rows(dscore * s_buf[half, quad, rows])
                p_buf[half, rows, lanes] = p.astype(BF16)
                ds_buf[half, rows, lanes] = (dscore * to_grad).astype(BF16)
            return jnp.sum(spread, axis=0, keepdims=True) * (SCALE * factor)

        def last(half):
            rows = key_rows(half)
            everyone = range(GROUP)
            turned_keys = jnp.transpose(kv[a, 0, rows])
            for quad in range(quads):
                ds = ds_buf[half, :, pl.ds(quad * LANES, LANES)]
                dq = jnp.dot(turned_keys, ds, preferred_element_type=F32).astype(BF16)
                dq = jnp.transpose(dq)
                for h in range(QUAD):
                    dq_buf[
                        a, late, pl.ds(half * HALF, HALF),
                        pl.ds((quad * QUAD + h) * HEAD_SIZE, HEAD_SIZE),
                    ] = dq[h * HALF:(h + 1) * HALF]
            acc[a, 0, rows] += jnp.dot(
                ds_buf[half], stack(0, half, everyone), preferred_element_type=F32
            )
            acc[a, 1, rows] += jnp.dot(
                p_buf[half], stack(1, half, everyone), preferred_element_type=F32
            )

        first(0, 0)
        first(0, 1)
        term00 = middle(0, 0)
        first(1, 0)
        term01 = middle(0, 1)
        first(1, 1)
        last(0)
        term10 = middle(1, 0)
        term11 = middle(1, 1)
        last(1)
        terms = [term00 + term10, term01 + term11]

        @pl.when(late == 0)
        def _():
            dq_own(a).start()
            for quad in range(quads):
                g_rows[quad] = terms[quad]

        @pl.when(late == 1)
        def _():
            for place in range(2):
                for which in range(2):
                    ret_send[a, place, which] = acc[a, which, pl.ds(place * BLOCK, BLOCK)].astype(BF16)
                back_copy(a, place).start()
            for quad in range(quads):
                both = g_rows[quad] + terms[quad]
                for side in range(2):
                    index = a * (2 * quads) + quad * 2 + side
                    piece = both[:, side * 2 * HALF:(side + 1) * 2 * HALF]
                    target = chips * core + index

                    @pl.when(target == me)
                    def _():
                        g_in1[chip] = piece

                    @pl.when(target != me)
                    def _():
                        g_part[index] = piece
                        gain_copy1(index).start()

            for which in range(2):
                mate_send[a, which] = acc[a, which, block(2 + other)].astype(BF16)
            mate_back(a).start()
            dq_mate(a).start()

        return carry

    lax.fori_loop(0, 4, step, 0)
    finish(0)

    def gain_arrive(i, carry):
        @pl.when(2 * i + lax.div(me, chips) != me)
        def _():
            remote(g_in1.at[i], g_in1.at[i], gain1_send.at[0], gain1_recv.at[i], mate).wait_recv()

        return carry

    lax.fori_loop(0, chips, gain_arrive, 0)
    g_sum[0] = jnp.sum(g_in1[...], axis=0)

    def gain_send2(i, carry):
        pltpu.make_async_remote_copy(
            src_ref=g_sum.at[0],
            dst_ref=g_in2.at[i - 1],
            send_sem=gain2_sem.at[0],
            recv_sem=gain2_sem.at[1],
            device_id={"dp": lax.rem(row + i, dp_size)},
            device_id_type=pl.DeviceIdType.MESH,
        ).start()
        return carry

    lax.fori_loop(1, dp_size, gain_send2, 0)
    finish(1)
    gain2_whole = remote(g_in2, g_in2, gain2_sem.at[0], gain2_sem.at[1], mate)
    gain2_whole.wait_recv()
    lanes = g_sum[0] + jnp.sum(g_in2[...], axis=0)
    lane1 = lax.broadcasted_iota(jnp.int32, (1, 2 * HALF), 1)
    gain_out[0] = jnp.sum(jnp.where(lane1 < HALF, lanes, 0.0))
    gain_out[1] = jnp.sum(jnp.where(lane1 < HALF, 0.0, lanes))

    gain2_whole.wait_send()

    def gain_left(index, carry):
        @pl.when(chips * core + index != me)
        def _():
            gain_copy1(index).wait_send()

        return carry

    lax.fori_loop(0, chips, gain_left, 0)
    for a in range(2):
        halo_whole(a).wait_send()
        mate_kv(a).wait_send()
        mate_qg(a).wait_send()
        back_whole(a).wait_send()
        mate_back(a).wait_send()
        dq_own(a).wait()
        dq_mate(a).wait_send()
        dq_from(a).wait_recv()
    for head in range(KEY_VALUE_HEADS):
        for which in range(2):
            dkv_out(head, which).wait()


def hand_over(dq_in, dk_in, dv_in, gain_in, dq_out, dk_out, dv_out, gain_to, dq_buf, dk_buf, dv_buf, gain_buf, sems):
    trips = [
        (dk_in, dk_buf, dk_out),
        (dv_in, dv_buf, dv_out),
        (gain_in, gain_buf, gain_to),
    ]
    for i in range(HAND_PARTS):
        rows = pl.ds(i * (BLOCK // HAND_PARTS), BLOCK // HAND_PARTS)
        trips.append((dq_in.at[rows], dq_buf.at[rows], dq_out.at[rows]))
    there = [pltpu.make_async_copy(x, y, sems.at[0, i]) for i, (x, y, _) in enumerate(trips)]
    back = [pltpu.make_async_copy(y, z, sems.at[1, i]) for i, (_, y, z) in enumerate(trips)]
    for copy in there:
        copy.start()
    for arrive, leave in zip(there, back):
        arrive.wait()
        leave.start()
    for copy in back:
        copy.wait()


def body(queries, keys, values, score_gain, grad, segment_ids):
    seq_size = lax.axis_size("seq")
    dp_size = lax.axis_size("dp")
    tokens = queries.shape[1]
    factor = 1.0 / (dp_size * tokens * seq_size)
    hbm = pl.BlockSpec(memory_space=pltpu.HBM)
    heads = KEY_VALUE_HEADS
    quads = GROUP // QUAD
    pair = pltpu.SemaphoreType.DMA((2,))
    wide = GROUP * HEAD_SIZE
    dq, dk, dv, gain = pl.pallas_call(
        functools.partial(kernel, seq_size, dp_size, factor),
        out_shape=(
            jax.ShapeDtypeStruct((BLOCK, QUERY_HEADS * HEAD_SIZE), BF16),
            jax.ShapeDtypeStruct((BLOCK, heads * HEAD_SIZE), BF16),
            jax.ShapeDtypeStruct((BLOCK, heads * HEAD_SIZE), BF16),
            jax.ShapeDtypeStruct((2,), F32),
        ),
        in_specs=[hbm] * 6,
        out_specs=(hbm, hbm, hbm, pl.BlockSpec(memory_space=pltpu.SMEM)),
        scratch_shapes=[
            pltpu.VMEM((2, 2, 2 * BLOCK, wide), BF16),
            pltpu.VMEM((2, 2, 4 * BLOCK, HEAD_SIZE), BF16),
            pltpu.VMEM((2, 2, 2, BLOCK, HEAD_SIZE), BF16),
            pltpu.VMEM((heads, 2, BLOCK, HEAD_SIZE), BF16),
            pltpu.VMEM((2, 2, BLOCK, HEAD_SIZE), BF16),
            pltpu.VMEM((2, 2, BLOCK, HEAD_SIZE), BF16),
            pltpu.VMEM((2, 2, 4 * BLOCK, HEAD_SIZE), F32),
            pltpu.VMEM((2, 2, BLOCK, wide), BF16),
            pltpu.VMEM((heads, 2, BLOCK, HEAD_SIZE), BF16),
            pltpu.VMEM((4 * BLOCK, BLOCK), F32),
            pltpu.VMEM((4, WINDOW, BLOCK), F32),
            pltpu.VMEM((2, quads, WINDOW, LANES), F32),
            pltpu.VMEM((2, quads, WINDOW, LANES), F32),
            pltpu.VMEM((2, quads, WINDOW, LANES), F32),
            pltpu.VMEM((2, WINDOW, quads * LANES), BF16),
            pltpu.VMEM((2, WINDOW, quads * LANES), BF16),
            pltpu.VMEM((1, tokens * seq_size), jnp.int32),
            pltpu.SMEM((QUERY_HEADS,), F32),
            pltpu.VMEM((quads, 1, LANES), F32),
            pltpu.VMEM((seq_size // 2, 1, 2 * HALF), F32),
            pltpu.VMEM((seq_size // 2, 1, 2 * HALF), F32),
            pltpu.VMEM((1, 1, 2 * HALF), F32),
            pltpu.VMEM((dp_size - 1, 1, 2 * HALF), F32),
            pair, pair, pair, pair, pair, pair, pair, pair,
            pair,
            pltpu.SemaphoreType.DMA((heads,)),
            pair, pair, pair, pair, pair,
            pltpu.SemaphoreType.DMA((heads, 2)),
            pltpu.SemaphoreType.DMA((seq_size // 2,)),
            pltpu.SemaphoreType.DMA((seq_size // 2,)),
            pair, pair,
        ],
        compiler_params=pltpu.CompilerParams(
            collective_id=0, has_side_effects=True, vmem_limit_bytes=VMEM_BYTES
        ),
        cost_estimate=pl.CostEstimate(
            flops=2 * 5 * BLOCK * WINDOW * HEAD_SIZE * QUERY_HEADS,
            bytes_accessed=4 * 1024 * 1024,
            transcendentals=BLOCK * WINDOW * QUERY_HEADS,
        ),
    )(queries[0], keys[0], values[0], score_gain, grad[0], segment_ids)
    results = (dq, dk, dv, gain)
    dq, dk, dv, gain = pl.pallas_call(
        hand_over,
        out_shape=tuple(jax.ShapeDtypeStruct(x.shape, x.dtype) for x in results),
        in_specs=[hbm] * 4,
        out_specs=(hbm,) * 4,
        scratch_shapes=[
            *[pltpu.VMEM(x.shape, x.dtype) for x in results[:3]],
            pltpu.SMEM(gain.shape, gain.dtype),
            pltpu.SemaphoreType.DMA((2, HAND_PARTS + 3)),
        ],
        compiler_params=pltpu.CompilerParams(vmem_limit_bytes=VMEM_BYTES),
    )(*results)
    return dq[None], dk[None], dv[None], gain


def solution(mesh):
    return jax.shard_map(
        body,
        mesh=mesh,
        in_specs=(
            P("dp", "seq", None),
            P("dp", "seq", None),
            P("dp", "seq", None),
            P(),
            P("dp", "seq", None),
            P("dp", None),
        ),
        out_specs=(P("dp", "seq", None), P("dp", "seq", None), P("dp", "seq", None), P("seq")),
        check_vma=False,
    )
```

time: 91.3 us -> 47 us (0.51)
  Pallas kernels: 90.6 us -> 46.2 us
    pallas_call x1, Pallas kernels: 40.9 us -> 2.17 us  [body(): pl.pallas_call(hand_over, out_shape=tuple((jax.ShapeDtypeStruct(x.shape,...]
    pallas_call x1, Pallas kernels: 49.7 us -> 44 us  [body(): pl.pallas_call(functools.partial(kernel, seq_size, dp_size, factor), out_...]
where the time goes in v2:
time: 47 us; the launch traced here: 46.8 us
  Pallas kernels  46.2 us (98%)
  between operations  0.64 us (1%)
    pallas_call x1, Pallas kernels, body(): pl.pallas_call(functools.partial(kernel, seq_size, dp_size, factor), out_...  44 us
    pallas_call x1, Pallas kernels, body(): pl.pallas_call(hand_over, out_shape=tuple((jax.ShapeDtypeStruct(x.shape,...  2.17 us

profile of v2, /device:TPU:24, one launch (start us, length us, event | category | flops | bytes accessed | tf_op | source)
XLA Modules:
  0.0 46.8 jit_solution(14017828300530897347)
XLA Ops:
  0.6 44.0 %shard_map.93 = (bf16[128,4096]{1,0:T(8,128)(2,1)}, bf16[128,512]{1,0:T(8,128)(2,1)}, bf16[128,512]{1,0:T(8,128)(2,1)}, f32[2]{0:T(128)}) custom-call(bf16[128,4096]{1,0:T(8,128)(2,1)} %bitcast.7, bf16[128,512]{1,0:T(8,128)(2,1)} %bitcast.10, bf16[128,512]{1,0:T(8,128)(2,1)} %bitcast.11, f32[32]{0:T(128)} %gain_hbm.1, bf16[128,4096]{1,0:T(8,128)(2,1)} %bitcast.8, ...), custom_call_target="tpu_custom_call" | custom-call | flops 1677721600 | bytes 4194304 | tf_op jit(solution)/shard_map/pallas_call | solution.py:460
  44.7 2.2 %shard_map.94 = (bf16[128,4096]{1,0:T(8,128)(2,1)}, bf16[128,512]{1,0:T(8,128)(2,1)}, bf16[128,512]{1,0:T(8,128)(2,1)}, f32[2]{0:T(128)}) custom-call(bf16[128,4096]{1,0:T(8,128)(2,1)} %get-tuple-element.12.dq_in, bf16[128,512]{1,0:T(8,128)(2,1)} %get-tuple-element.13.dk_in, bf16[128,512]{1,0:T(8,128)(2,1)} %get-tuple-element.14.dv_in, ...), custom_call_target="tpu_custom_call" | custom-call | tf_op jit(solution)/shard_map/pallas_call | solution.py:513

commit v3 on v2

--- a/solution.py
+++ b/solution.py
@@ -76,7 +76,7 @@
 
     def greet_seq(i, carry):
         pl.semaphore_signal(
-            barrier, inc=1, device_id={"seq": lax.rem(me + i, seq_size)}, device_id_type=pl.DeviceIdType.MESH
+            barrier, inc=1, device_id={"seq": lax.rem(me - i + seq_size, seq_size)}, device_id_type=pl.DeviceIdType.MESH
         )
         return carry
 
@@ -102,26 +102,26 @@
     pl.semaphore_wait(barrier, seq_size + dp_size - 2)
 
     def halo_start(a):
-        for to_core in range(2):
-            for which, source in enumerate((k_hbm, v_hbm)):
+        for which, source in enumerate((k_hbm, v_hbm)):
+            for to_core in range(2):
                 remote(
                     source.at[:, thin(2 * to_core + a)],
                     kv.at[a, which, block(core)],
-                    halo_send.at[a],
-                    halo_recv.at[a],
+                    halo_send.at[a, which],
+                    halo_recv.at[a, which],
                     2 * next_chip + to_core,
                 ).start()
 
-    def halo_whole(a):
-        part = kv.at[a, :, pl.ds(0, 2 * BLOCK)]
-        return remote(part, part, halo_send.at[a], halo_recv.at[a], 2 * next_chip)
+    def halo_whole(a, which):
+        part = kv.at[a, which, pl.ds(0, 2 * BLOCK)]
+        return remote(part, part, halo_send.at[a, which], halo_recv.at[a, which], 2 * next_chip)
 
     def mate_start(a):
         head = 2 * other + a
         for which, source in enumerate((k_hbm, v_hbm)):
             remote(
                 source.at[:, thin(head)], kv.at[a, which, block(2 + core)],
-                mate_kv_send.at[a], mate_kv_recv.at[a], mate,
+                mate_kv_send.at[a, which], mate_kv_recv.at[a, which], mate,
             ).start()
         for which, source in enumerate((q_hbm, g_hbm)):
             remote(
@@ -129,9 +129,9 @@
                 mate_qg_send.at[a], mate_qg_recv.at[a], mate,
             ).start()
 
-    def mate_kv(a):
-        part = kv.at[a, :, block(2 + other)]
-        return remote(part, part, mate_kv_send.at[a], mate_kv_recv.at[a], mate)
+    def mate_kv(a, which):
+        part = kv.at[a, which, block(2 + other)]
+        return remote(part, part, mate_kv_send.at[a, which], mate_kv_recv.at[a, which], mate)
 
     def mate_qg(a):
         part = qg.at[a, :, block(other)]
@@ -140,6 +140,7 @@
     halo_start(0)
     mate_start(0)
     mate_start(1)
+    acc[...] = jnp.zeros(acc.shape, F32)
     seg_copy.wait()
     gain_copy.wait()
 
@@ -223,48 +224,41 @@
             g_part.at[index], g_in1.at[chip], gain1_send.at[index], gain1_recv.at[chip], chips * core + index
         )
 
-    def step(number, carry):
+    def block_of(late):
+        return core + late - 2 * core * late
+
+    def key_rows(x, half):
+        return pl.ds(pl.multiple_of(x * BLOCK + half * HALF, HALF), WINDOW)
+
+    def stack(a, x, which, half, heads):
+        rows = pl.ds(pl.multiple_of(x * BLOCK + half * HALF, HALF), HALF)
+        return jnp.concatenate(
+            [qg[a, which, rows, pl.ds(h * HEAD_SIZE, HEAD_SIZE)] for h in heads], axis=0
+        )
+
+    def scores(number, carry):
         a = lax.div(number, 2)
         late = number - 2 * a
-        x = core + late - 2 * core * late
-        base = x * BLOCK
+        x = block_of(late)
 
         @pl.when(late == 0)
         def _():
-            halo_whole(a).wait_recv()
-
-            @pl.when(a == 0)
-            def _():
-                halo_start(1)
-
             own = kv.at[a, :, block(2 + core)]
             pltpu.make_async_copy(own, own, own_sem.at[a]).wait()
             held = qg.at[a, :, block(core)]
             pltpu.make_async_copy(held, held, in_sem.at[a]).wait()
-            mate_kv(a).wait_recv()
-            acc[a] = jnp.zeros((2, 4 * BLOCK, HEAD_SIZE), F32)
+            mate_kv(a, 0).wait_recv()
+            halo_whole(a, 0).wait_recv()
 
         @pl.when(late == 1)
         def _():
             mate_qg(a).wait_recv()
 
-        def key_rows(half):
-            return pl.ds(pl.multiple_of(base + half * HALF, HALF), WINDOW)
-
-        def stack(which, half, heads):
-            rows = pl.ds(pl.multiple_of(base + half * HALF, HALF), HALF)
-            return jnp.concatenate(
-                [qg[a, which, rows, pl.ds(h * HEAD_SIZE, HEAD_SIZE)] for h in heads], axis=0
-            )
-
-        def first(half, quad):
-            rows = key_rows(half)
+        def product(target, which, half, quad):
             heads = range(quad * QUAD, quad * QUAD + QUAD)
-            s_buf[half, quad] = lax.dot_general(
-                kv[a, 0, rows], stack(0, half, heads), NT, preferred_element_type=F32
-            )
-            dp_buf[half, quad] = lax.dot_general(
-                kv[a, 1, rows], stack(1, half, heads), NT, preferred_element_type=F32
+            target[half, quad] = lax.dot_general(
+                kv[a, which, key_rows(x, half)], stack(a, x, which, half, heads), NT,
+                preferred_element_type=F32,
             )
 
         def middle(half, quad):
@@ -299,54 +293,41 @@
                 p = y_buf[half, quad, rows] * inverse
                 dscore = p * (dp_buf[half, quad, rows] - delta)
                 spread = spread + fold_rows(dscore * s_buf[half, quad, rows])
-                p_buf[half, rows, lanes] = p.astype(BF16)
-                ds_buf[half, rows, lanes] = (dscore * to_grad).astype(BF16)
+                p_buf[number, half, rows, lanes] = p.astype(BF16)
+                ds_buf[number, half, rows, lanes] = (dscore * to_grad).astype(BF16)
             return jnp.sum(spread, axis=0, keepdims=True) * (SCALE * factor)
 
-        def last(half):
-            rows = key_rows(half)
-            everyone = range(GROUP)
-            turned_keys = jnp.transpose(kv[a, 0, rows])
-            for quad in range(quads):
-                ds = ds_buf[half, :, pl.ds(quad * LANES, LANES)]
-                dq = jnp.dot(turned_keys, ds, preferred_element_type=F32).astype(BF16)
-                dq = jnp.transpose(dq)
-                for h in range(QUAD):
-                    dq_buf[
-                        a, late, pl.ds(half * HALF, HALF),
-                        pl.ds((quad * QUAD + h) * HEAD_SIZE, HEAD_SIZE),
-                    ] = dq[h * HALF:(h + 1) * HALF]
-            acc[a, 0, rows] += jnp.dot(
-                ds_buf[half], stack(0, half, everyone), preferred_element_type=F32
-            )
-            acc[a, 1, rows] += jnp.dot(
-                p_buf[half], stack(1, half, everyone), preferred_element_type=F32
-            )
-
-        first(0, 0)
-        first(0, 1)
+        product(s_buf, 0, 0, 0)
+        product(s_buf, 0, 0, 1)
+        product(s_buf, 0, 1, 0)
+        product(s_buf, 0, 1, 1)
+
+        @pl.when(late == 0)
+        def _():
+            mate_kv(a, 1).wait_recv()
+            halo_whole(a, 1).wait_recv()
+
+            @pl.when(a == 0)
+            def _():
+                halo_start(1)
+
+        product(dp_buf, 1, 0, 0)
+        product(dp_buf, 1, 0, 1)
         term00 = middle(0, 0)
-        first(1, 0)
+        product(dp_buf, 1, 1, 0)
         term01 = middle(0, 1)
-        first(1, 1)
-        last(0)
+        product(dp_buf, 1, 1, 1)
         term10 = middle(1, 0)
         term11 = middle(1, 1)
-        last(1)
         terms = [term00 + term10, term01 + term11]
 
         @pl.when(late == 0)
         def _():
-            dq_own(a).start()
             for quad in range(quads):
                 g_rows[quad] = terms[quad]
 
         @pl.when(late == 1)
         def _():
-            for place in range(2):
-                for which in range(2):
-                    ret_send[a, place, which] = acc[a, which, pl.ds(place * BLOCK, BLOCK)].astype(BF16)
-                back_copy(a, place).start()
             for quad in range(quads):
                 both = g_rows[quad] + terms[quad]
                 for side in range(2):
@@ -363,15 +344,9 @@
                         g_part[index] = piece
                         gain_copy1(index).start()
 
-            for which in range(2):
-                mate_send[a, which] = acc[a, which, block(2 + other)].astype(BF16)
-            mate_back(a).start()
-            dq_mate(a).start()
-
-        return carry
-
-    lax.fori_loop(0, 4, step, 0)
-    finish(0)
+        return carry
+
+    lax.fori_loop(0, 4, scores, 0)
 
     def gain_arrive(i, carry):
         @pl.when(2 * i + lax.div(me, chips) != me)
@@ -395,6 +370,53 @@
         return carry
 
     lax.fori_loop(1, dp_size, gain_send2, 0)
+
+    def key_side(a, carry):
+        for late in range(2):
+            x = block_of(late)
+            for half in range(2):
+                rows = key_rows(x, half)
+                acc[a, 0, rows] += jnp.dot(
+                    ds_buf[2 * a + late, half], stack(a, x, 0, half, range(GROUP)),
+                    preferred_element_type=F32,
+                )
+                acc[a, 1, rows] += jnp.dot(
+                    p_buf[2 * a + late, half], stack(a, x, 1, half, range(GROUP)),
+                    preferred_element_type=F32,
+                )
+        for place in range(2):
+            for which in range(2):
+                ret_send[a, place, which] = acc[a, which, pl.ds(place * BLOCK, BLOCK)].astype(BF16)
+            back_copy(a, place).start()
+        for which in range(2):
+            mate_send[a, which] = acc[a, which, block(2 + other)].astype(BF16)
+        mate_back(a).start()
+        return carry
+
+    lax.fori_loop(0, 2, key_side, 0)
+
+    def query_side(a, carry):
+        for late in (1, 0):
+            x = block_of(late)
+            for half in range(2):
+                turned_keys = jnp.transpose(kv[a, 0, key_rows(x, half)])
+                for quad in range(quads):
+                    ds = ds_buf[2 * a + late, half, :, pl.ds(quad * LANES, LANES)]
+                    dq = jnp.dot(turned_keys, ds, preferred_element_type=F32).astype(BF16)
+                    dq = jnp.transpose(dq)
+                    for h in range(QUAD):
+                        dq_buf[
+                            a, late, pl.ds(half * HALF, HALF),
+                            pl.ds((quad * QUAD + h) * HEAD_SIZE, HEAD_SIZE),
+                        ] = dq[h * HALF:(h + 1) * HALF]
+            if late:
+                dq_mate(a).start()
+            else:
+                dq_own(a).start()
+        return carry
+
+    lax.fori_loop(0, 2, query_side, 0)
+    finish(0)
     finish(1)
     gain2_whole = remote(g_in2, g_in2, gain2_sem.at[0], gain2_sem.at[1], mate)
     gain2_whole.wait_recv()
@@ -414,8 +436,9 @@
 
     lax.fori_loop(0, chips, gain_left, 0)
     for a in range(2):
-        halo_whole(a).wait_send()
-        mate_kv(a).wait_send()
+        for which in range(2):
+            halo_whole(a, which).wait_send()
+            mate_kv(a, which).wait_send()
         mate_qg(a).wait_send()
         back_whole(a).wait_send()
         mate_back(a).wait_send()
@@ -456,6 +479,7 @@
     heads = KEY_VALUE_HEADS
     quads = GROUP // QUAD
     pair = pltpu.SemaphoreType.DMA((2,))
+    four = pltpu.SemaphoreType.DMA((2, 2))
     wide = GROUP * HEAD_SIZE
     dq, dk, dv, gain = pl.pallas_call(
         functools.partial(kernel, seq_size, dp_size, factor),
@@ -482,8 +506,8 @@
             pltpu.VMEM((2, quads, WINDOW, LANES), F32),
             pltpu.VMEM((2, quads, WINDOW, LANES), F32),
             pltpu.VMEM((2, quads, WINDOW, LANES), F32),
-            pltpu.VMEM((2, WINDOW, quads * LANES), BF16),
-            pltpu.VMEM((2, WINDOW, quads * LANES), BF16),
+            pltpu.VMEM((4, 2, WINDOW, quads * LANES), BF16),
+            pltpu.VMEM((4, 2, WINDOW, quads * LANES), BF16),
             pltpu.VMEM((1, tokens * seq_size), jnp.int32),
             pltpu.SMEM((QUERY_HEADS,), F32),
             pltpu.VMEM((quads, 1, LANES), F32),
@@ -491,7 +515,7 @@
             pltpu.VMEM((seq_size // 2, 1, 2 * HALF), F32),
             pltpu.VMEM((1, 1, 2 * HALF), F32),
             pltpu.VMEM((dp_size - 1, 1, 2 * HALF), F32),
-            pair, pair, pair, pair, pair, pair, pair, pair,
+            pair, pair, four, four, four, four, pair, pair,
             pair,
             pltpu.SemaphoreType.DMA((heads,)),
             pair, pair, pair, pair, pair,

time: 47 us -> 47.2 us (level)
  the two profiles are of different devices: /device:TPU:24 before, /device:TPU:9 now
where the time goes in v3:
time: 47.2 us; the launch traced here: 47 us
  Pallas kernels  46.4 us (98%)
  between operations  0.64 us (1%)
    pallas_call x1, Pallas kernels, body(): pl.pallas_call(functools.partial(kernel, seq_size, dp_size, factor), out_...  44.2 us
    pallas_call x1, Pallas kernels, body(): pl.pallas_call(hand_over, out_shape=tuple((jax.ShapeDtypeStruct(x.shape,...  2.17 us

profile of v3, /device:TPU:9, one launch (start us, length us, event | category | flops | bytes accessed | tf_op | source)
XLA Modules:
  0.0 47.0 jit_solution(2436773260895184217)
XLA Ops:
  0.6 44.2 %shard_map.93 = (bf16[128,4096]{1,0:T(8,128)(2,1)}, bf16[128,512]{1,0:T(8,128)(2,1)}, bf16[128,512]{1,0:T(8,128)(2,1)}, f32[2]{0:T(128)}) custom-call(bf16[128,4096]{1,0:T(8,128)(2,1)} %bitcast.7, bf16[128,512]{1,0:T(8,128)(2,1)} %bitcast.10, bf16[128,512]{1,0:T(8,128)(2,1)} %bitcast.11, f32[32]{0:T(128)} %gain_hbm.1, bf16[128,4096]{1,0:T(8,128)(2,1)} %bitcast.8, ...), custom_call_target="tpu_custom_call" | custom-call | flops 1677721600 | bytes 4194304 | tf_op jit(solution)/shard_map/pallas_call | solution.py:484
  44.9 2.2 %shard_map.94 = (bf16[128,4096]{1,0:T(8,128)(2,1)}, bf16[128,512]{1,0:T(8,128)(2,1)}, bf16[128,512]{1,0:T(8,128)(2,1)}, f32[2]{0:T(128)}) custom-call(bf16[128,4096]{1,0:T(8,128)(2,1)} %get-tuple-element.12.dq_in, bf16[128,512]{1,0:T(8,128)(2,1)} %get-tuple-element.13.dk_in, bf16[128,512]{1,0:T(8,128)(2,1)} %get-tuple-element.14.dv_in, ...), custom_call_target="tpu_custom_call" | custom-call | tf_op jit(solution)/shard_map/pallas_call | solution.py:537

commit v4 on v3

--- a/solution.py
+++ b/solution.py
@@ -19,6 +19,7 @@
 LANES = QUAD * HALF
 CHUNK = 64
 HAND_PARTS = 4
+LEADER = 7
 VMEM_BYTES = 64 * 1024 * 1024
 LOG2E = math.log2(math.e)
 SCALE = HEAD_SIZE ** -0.5
@@ -38,10 +39,10 @@
     dq_hbm, dk_hbm, dv_hbm, gain_out,
     qg, kv, ret_send, ret, mate_send, mate_in, acc, dq_buf, dkv_buf, seg_rows, bias,
     s_buf, dp_buf, y_buf, p_buf, ds_buf, seg_ref, gain_ref,
-    g_rows, g_part, g_in1, g_sum, g_in2,
+    g_rows, g_part, g_in1, g_sum, g_in2, g_total,
     in_sem, own_sem, halo_send, halo_recv, mate_kv_send, mate_kv_recv, mate_qg_send, mate_qg_recv,
     back_send, back_recv, mate_back_send, mate_back_recv, dq_sem, mate_dq_send, mate_dq_recv,
-    dkv_sem, gain1_send, gain1_recv, gain2_sem, small_sem,
+    dkv_sem, gain1_send, gain1_recv, gain2_sem, gain3_sem, small_sem, ready,
 ):
     me = lax.axis_index("seq")
     row = lax.axis_index("dp")
@@ -75,9 +76,14 @@
     barrier = pltpu.get_barrier_semaphore()
 
     def greet_seq(i, carry):
-        pl.semaphore_signal(
-            barrier, inc=1, device_id={"seq": lax.rem(me - i + seq_size, seq_size)}, device_id_type=pl.DeviceIdType.MESH
-        )
+        there = lax.rem(me - i + seq_size, seq_size)
+
+        @pl.when(there != LEADER)
+        def _():
+            pl.semaphore_signal(
+                barrier, inc=1, device_id={"seq": there}, device_id_type=pl.DeviceIdType.MESH
+            )
+
         return carry
 
     def greet_dp(i, carry):
@@ -87,7 +93,10 @@
         return carry
 
     lax.fori_loop(1, seq_size, greet_seq, 0)
-    lax.fori_loop(1, dp_size, greet_dp, 0)
+
+    @pl.when(me == LEADER)
+    def _():
+        lax.fori_loop(1, dp_size, greet_dp, 0)
 
     for a in range(2):
         head = 2 * core + a
@@ -99,7 +108,17 @@
     gain_copy = pltpu.make_async_copy(gain_hbm, gain_ref, small_sem.at[1])
     seg_copy.start()
     gain_copy.start()
-    pl.semaphore_wait(barrier, seq_size + dp_size - 2)
+
+    @pl.when(me != LEADER)
+    def _():
+        pl.semaphore_wait(barrier, seq_size - 1)
+        pl.semaphore_signal(
+            ready, inc=1, device_id={"seq": LEADER}, device_id_type=pl.DeviceIdType.MESH
+        )
+
+    @pl.when(me == LEADER)
+    def _():
+        pl.semaphore_wait(ready, seq_size - 1)
 
     def halo_start(a):
         for which, source in enumerate((k_hbm, v_hbm)):
@@ -219,10 +238,11 @@
         part = dq_hbm.at[:, wide(2 * other + a)]
         return remote(part, part, mate_dq_send.at[a], mate_dq_recv.at[a], mate)
 
-    def gain_copy1(index):
-        return remote(
-            g_part.at[index], g_in1.at[chip], gain1_send.at[index], gain1_recv.at[chip], chips * core + index
-        )
+    def gain_copy1(source):
+        return remote(g_part, g_in1.at[source], gain1_send.at[0], gain1_recv.at[source], LEADER)
+
+    def gain_copy3(target):
+        return remote(g_total.at[0], g_total.at[1], gain3_sem.at[0], gain3_sem.at[1], target)
 
     def block_of(late):
         return core + late - 2 * core * late
@@ -332,31 +352,22 @@
                 both = g_rows[quad] + terms[quad]
                 for side in range(2):
                     index = a * (2 * quads) + quad * 2 + side
-                    piece = both[:, side * 2 * HALF:(side + 1) * 2 * HALF]
-                    target = chips * core + index
-
-                    @pl.when(target == me)
-                    def _():
-                        g_in1[chip] = piece
-
-                    @pl.when(target != me)
-                    def _():
-                        g_part[index] = piece
-                        gain_copy1(index).start()
+                    g_part[pl.ds(index, 1), :] = both[:, side * 2 * HALF:(side + 1) * 2 * HALF]
 
         return carry
 
     lax.fori_loop(0, 4, scores, 0)
 
+    @pl.when(me != LEADER)
+    def _():
+        gain_copy1(me).start()
+
     def gain_arrive(i, carry):
-        @pl.when(2 * i + lax.div(me, chips) != me)
+        @pl.when(i != LEADER)
         def _():
-            remote(g_in1.at[i], g_in1.at[i], gain1_send.at[0], gain1_recv.at[i], mate).wait_recv()
-
-        return carry
-
-    lax.fori_loop(0, chips, gain_arrive, 0)
-    g_sum[0] = jnp.sum(g_in1[...], axis=0)
+            gain_copy1(i).wait_recv()
+
+        return carry
 
     def gain_send2(i, carry):
         pltpu.make_async_remote_copy(
@@ -369,7 +380,24 @@
         ).start()
         return carry
 
-    lax.fori_loop(1, dp_size, gain_send2, 0)
+    @pl.when(me == LEADER)
+    def _():
+        g_in1[LEADER] = g_part[...]
+        lax.fori_loop(0, seq_size, gain_arrive, 0)
+        pairs = lax.broadcasted_iota(jnp.int32, (chips, 2 * HALF), 0)
+        lanes = lax.broadcasted_iota(jnp.int32, (chips, 2 * HALF), 1)
+        sums = jnp.zeros((chips, 2 * HALF), F32)
+        for side in range(2):
+            held = g_in1[side]
+            for i in range(1, chips):
+                held = held + g_in1[2 * i + side]
+            low = jnp.sum(jnp.where(lanes < HALF, held, 0.0), axis=1, keepdims=True)
+            high = jnp.sum(jnp.where(lanes < HALF, 0.0, held), axis=1, keepdims=True)
+            place = 2 * (pairs + chips * side)
+            sums = sums + jnp.where(lanes == place, low, 0.0) + jnp.where(lanes == place + 1, high, 0.0)
+        g_sum[0] = jnp.sum(sums, axis=0, keepdims=True)
+        pl.semaphore_wait(barrier, dp_size - 1)
+        lax.fori_loop(1, dp_size, gain_send2, 0)
 
     def key_side(a, carry):
         for late in range(2):
@@ -419,22 +447,36 @@
     finish(0)
     finish(1)
     gain2_whole = remote(g_in2, g_in2, gain2_sem.at[0], gain2_sem.at[1], mate)
-    gain2_whole.wait_recv()
-    lanes = g_sum[0] + jnp.sum(g_in2[...], axis=0)
+
+    def gain_send3(i, carry):
+        gain_copy3(lax.rem(me + i, seq_size)).start()
+        return carry
+
+    @pl.when(me == LEADER)
+    def _():
+        gain2_whole.wait_recv()
+        g_total[0] = g_sum[0] + jnp.sum(g_in2[...], axis=0)
+        lax.fori_loop(1, seq_size, gain_send3, 0)
+        g_total[1] = g_total[0]
+
+    @pl.when(me != LEADER)
+    def _():
+        gain_copy3(mate).wait_recv()
+
     lane1 = lax.broadcasted_iota(jnp.int32, (1, 2 * HALF), 1)
-    gain_out[0] = jnp.sum(jnp.where(lane1 < HALF, lanes, 0.0))
-    gain_out[1] = jnp.sum(jnp.where(lane1 < HALF, 0.0, lanes))
-
-    gain2_whole.wait_send()
-
-    def gain_left(index, carry):
-        @pl.when(chips * core + index != me)
-        def _():
-            gain_copy1(index).wait_send()
-
-        return carry
-
-    lax.fori_loop(0, chips, gain_left, 0)
+    for side in range(2):
+        gain_out[side] = jnp.sum(jnp.where(lane1 == 2 * me + side, g_total[1], 0.0))
+
+    @pl.when(me == LEADER)
+    def _():
+        gain2_whole.wait_send()
+        sent = g_in2.at[pl.ds(0, seq_size - 1)]
+        remote(sent, sent, gain3_sem.at[0], gain3_sem.at[1], mate).wait_send()
+
+    @pl.when(me != LEADER)
+    def _():
+        gain_copy1(me).wait_send()
+
     for a in range(2):
         for which in range(2):
             halo_whole(a, which).wait_send()
@@ -511,18 +553,20 @@
             pltpu.VMEM((1, tokens * seq_size), jnp.int32),
             pltpu.SMEM((QUERY_HEADS,), F32),
             pltpu.VMEM((quads, 1, LANES), F32),
-            pltpu.VMEM((seq_size // 2, 1, 2 * HALF), F32),
-            pltpu.VMEM((seq_size // 2, 1, 2 * HALF), F32),
+            pltpu.VMEM((seq_size // 2, 2 * HALF), F32),
+            pltpu.VMEM((seq_size, seq_size // 2, 2 * HALF), F32),
             pltpu.VMEM((1, 1, 2 * HALF), F32),
             pltpu.VMEM((dp_size - 1, 1, 2 * HALF), F32),
+            pltpu.VMEM((2, 1, 2 * HALF), F32),
             pair, pair, four, four, four, four, pair, pair,
             pair,
             pltpu.SemaphoreType.DMA((heads,)),
             pair, pair, pair, pair, pair,
             pltpu.SemaphoreType.DMA((heads, 2)),
-            pltpu.SemaphoreType.DMA((seq_size // 2,)),
-            pltpu.SemaphoreType.DMA((seq_size // 2,)),
-            pair, pair,
+            pair,
+            pltpu.SemaphoreType.DMA((seq_size,)),
+            pair, pair, pair,
+            pltpu.SemaphoreType.REGULAR,
         ],
         compiler_params=pltpu.CompilerParams(
             collective_id=0, has_side_effects=True, vmem_limit_bytes=VMEM_BYTES

time: 47.2 us -> 44.1 us (0.934)
  the two profiles are of different devices: /device:TPU:9 before, /device:TPU:1 now
where the time goes in v4:
time: 44.1 us; the launch traced here: 44 us
  Pallas kernels  43.3 us (98%)
  between operations  0.64 us (1%)
    pallas_call x1, Pallas kernels, body(): pl.pallas_call(functools.partial(kernel, seq_size, dp_size, factor), out_...  41.1 us
    pallas_call x1, Pallas kernels, body(): pl.pallas_call(hand_over, out_shape=tuple((jax.ShapeDtypeStruct(x.shape,...  2.17 us

profile of v4, /device:TPU:1, one launch (start us, length us, event | category | flops | bytes accessed | tf_op | source)
XLA Modules:
  0.0 44.0 jit_solution(6640522940667222540)
XLA Ops:
  0.6 41.1 %shard_map.93 = (bf16[128,4096]{1,0:T(8,128)(2,1)}, bf16[128,512]{1,0:T(8,128)(2,1)}, bf16[128,512]{1,0:T(8,128)(2,1)}, f32[2]{0:T(128)}) custom-call(bf16[128,4096]{1,0:T(8,128)(2,1)} %bitcast.7, bf16[128,512]{1,0:T(8,128)(2,1)} %bitcast.10, bf16[128,512]{1,0:T(8,128)(2,1)} %bitcast.11, f32[32]{0:T(128)} %gain_hbm.1, bf16[128,4096]{1,0:T(8,128)(2,1)} %bitcast.8, ...), custom_call_target="tpu_custom_call" | custom-call | flops 1677721600 | bytes 4194304 | tf_op jit(solution)/shard_map/pallas_call | solution.py:526
  41.8 2.2 %shard_map.94 = (bf16[128,4096]{1,0:T(8,128)(2,1)}, bf16[128,512]{1,0:T(8,128)(2,1)}, bf16[128,512]{1,0:T(8,128)(2,1)}, f32[2]{0:T(128)}) custom-call(bf16[128,4096]{1,0:T(8,128)(2,1)} %get-tuple-element.12.dq_in, bf16[128,512]{1,0:T(8,128)(2,1)} %get-tuple-element.13.dk_in, bf16[128,512]{1,0:T(8,128)(2,1)} %get-tuple-element.14.dv_in, ...), custom_call_target="tpu_custom_call" | custom-call | tf_op jit(solution)/shard_map/pallas_call | solution.py:581

commit v5 on v4

--- a/solution.py
+++ b/solution.py
@@ -13,11 +13,12 @@
 HEAD_SIZE = 128
 GROUP = QUERY_HEADS // KEY_VALUE_HEADS
 BLOCK = 128
-HALF = 64
-WINDOW = 320
-QUAD = 4
-LANES = QUAD * HALF
-CHUNK = 64
+PART = 32
+PARTS = BLOCK // PART
+WINDOW = 288
+LANES = GROUP * PART
+SIDE = 128
+CHUNK = 32
 HAND_PARTS = 4
 LEADER = 7
 VMEM_BYTES = 64 * 1024 * 1024
@@ -39,7 +40,7 @@
     dq_hbm, dk_hbm, dv_hbm, gain_out,
     qg, kv, ret_send, ret, mate_send, mate_in, acc, dq_buf, dkv_buf, seg_rows, bias,
     s_buf, dp_buf, y_buf, p_buf, ds_buf, seg_ref, gain_ref,
-    g_rows, g_part, g_in1, g_sum, g_in2, g_total,
+    g_part, g_in1, g_sum, g_in2, g_total,
     in_sem, own_sem, halo_send, halo_recv, mate_kv_send, mate_kv_recv, mate_qg_send, mate_qg_recv,
     back_send, back_recv, mate_back_send, mate_back_recv, dq_sem, mate_dq_send, mate_dq_recv,
     dkv_sem, gain1_send, gain1_recv, gain2_sem, gain3_sem, small_sem, ready,
@@ -102,8 +103,8 @@
         head = 2 * core + a
         pltpu.make_async_copy(k_hbm.at[:, thin(head)], kv.at[a, 0, block(2 + core)], own_sem.at[a]).start()
         pltpu.make_async_copy(v_hbm.at[:, thin(head)], kv.at[a, 1, block(2 + core)], own_sem.at[a]).start()
-        pltpu.make_async_copy(q_hbm.at[:, wide(head)], qg.at[a, 0, block(core)], in_sem.at[a]).start()
-        pltpu.make_async_copy(g_hbm.at[:, wide(head)], qg.at[a, 1, block(core)], in_sem.at[a]).start()
+        pltpu.make_async_copy(q_hbm.at[:, wide(head)], qg.at[a, 0, pl.ds(0, BLOCK)], in_sem.at[a]).start()
+        pltpu.make_async_copy(g_hbm.at[:, wide(head)], qg.at[a, 1, pl.ds(0, BLOCK)], in_sem.at[a]).start()
     seg_copy = pltpu.make_async_copy(seg_hbm, seg_ref, small_sem.at[0])
     gain_copy = pltpu.make_async_copy(gain_hbm, gain_ref, small_sem.at[1])
     seg_copy.start()
@@ -144,7 +145,7 @@
             ).start()
         for which, source in enumerate((q_hbm, g_hbm)):
             remote(
-                source.at[:, wide(head)], qg.at[a, which, block(core)],
+                source.at[:, wide(head)], qg.at[a, which, pl.ds(BLOCK, BLOCK)],
                 mate_qg_send.at[a], mate_qg_recv.at[a], mate,
             ).start()
 
@@ -153,7 +154,7 @@
         return remote(part, part, mate_kv_send.at[a, which], mate_kv_recv.at[a, which], mate)
 
     def mate_qg(a):
-        part = qg.at[a, :, block(other)]
+        part = qg.at[a, :, pl.ds(BLOCK, BLOCK)]
         return remote(part, part, mate_qg_send.at[a], mate_qg_recv.at[a], mate)
 
     halo_start(0)
@@ -171,22 +172,28 @@
         seg_rows[pl.ds(b * BLOCK, BLOCK)] = jnp.transpose(
             jnp.broadcast_to(ids_of(b - 2), (BLOCK, BLOCK))
         )
-    lane8 = lax.broadcasted_iota(jnp.int32, (8, BLOCK), 1)
+    def block_of(late):
+        return other if late else core
+
+    group8 = lax.broadcasted_iota(jnp.int32, (8, BLOCK), 1) // PART
     key_place = lax.broadcasted_iota(jnp.int32, (WINDOW, BLOCK), 0)
     lane = lax.broadcasted_iota(jnp.int32, (WINDOW, BLOCK), 1)
-    causal = key_place <= 2 * BLOCK + jnp.where(lane < HALF, lane, lane - HALF)
-    for x in range(2):
+    causal = key_place <= 2 * BLOCK + lane % PART
+    for late in range(2):
+        x = block_of(late)
         query_ids = jnp.broadcast_to(ids_of(x), (8, BLOCK))
-        turned = pltpu.roll(query_ids, HALF, 1)
-        for half in range(2):
-            start = x * BLOCK + half * HALF
-            ids = jnp.where((lane8 < HALF) == (half == 0), query_ids, turned)[0:1]
+        rolled = [query_ids] + [pltpu.roll(query_ids, PART * k, 1) for k in range(1, PARTS)]
+        for part in range(PARTS):
+            start = x * BLOCK + part * PART
+            ids = rolled[-part % PARTS]
+            for j in range(1, PARTS):
+                ids = jnp.where(group8 == j, rolled[(j - part) % PARTS], ids)
             inside = (chip - 1) * (2 * BLOCK) + start + key_place >= 0
-            allowed = (seg_rows[pl.ds(start, WINDOW)] == ids) & causal & inside
-            bias[2 * x + half] = jnp.where(allowed, 0.0, -1e30)
+            keys_ids = seg_rows[pl.ds(pl.multiple_of(start, PART), WINDOW)]
+            allowed = (keys_ids == ids[0:1]) & causal & inside
+            bias[late * PARTS + part] = jnp.where(allowed, 0.0, -1e30)
 
     lane_wide = lax.broadcasted_iota(jnp.int32, (1, LANES), 1)
-    quads = GROUP // QUAD
 
     def back_copy(a, place):
         return remote(
@@ -244,119 +251,89 @@
     def gain_copy3(target):
         return remote(g_total.at[0], g_total.at[1], gain3_sem.at[0], gain3_sem.at[1], target)
 
-    def block_of(late):
-        return core + late - 2 * core * late
-
-    def key_rows(x, half):
-        return pl.ds(pl.multiple_of(x * BLOCK + half * HALF, HALF), WINDOW)
-
-    def stack(a, x, which, half, heads):
-        rows = pl.ds(pl.multiple_of(x * BLOCK + half * HALF, HALF), HALF)
+    def key_rows(late, part):
+        return pl.ds(pl.multiple_of(block_of(late) * BLOCK + part * PART, PART), WINDOW)
+
+    def stack(a, late, which, part):
+        rows = pl.ds(late * BLOCK + part * PART, PART)
         return jnp.concatenate(
-            [qg[a, which, rows, pl.ds(h * HEAD_SIZE, HEAD_SIZE)] for h in heads], axis=0
-        )
-
-    def scores(number, carry):
-        a = lax.div(number, 2)
-        late = number - 2 * a
-        x = block_of(late)
-
-        @pl.when(late == 0)
-        def _():
-            own = kv.at[a, :, block(2 + core)]
-            pltpu.make_async_copy(own, own, own_sem.at[a]).wait()
-            held = qg.at[a, :, block(core)]
-            pltpu.make_async_copy(held, held, in_sem.at[a]).wait()
-            mate_kv(a, 0).wait_recv()
-            halo_whole(a, 0).wait_recv()
-
-        @pl.when(late == 1)
-        def _():
-            mate_qg(a).wait_recv()
-
-        def product(target, which, half, quad):
-            heads = range(quad * QUAD, quad * QUAD + QUAD)
-            target[half, quad] = lax.dot_general(
-                kv[a, which, key_rows(x, half)], stack(a, x, which, half, heads), NT,
+            [qg[a, which, rows, pl.ds(h * HEAD_SIZE, HEAD_SIZE)] for h in range(GROUP)], axis=0
+        )
+
+    units = [(late, part) for late in range(2) for part in range(PARTS)]
+
+    def scores(a, carry):
+        gain = jnp.full((1, LANES), gain_ref[(2 * core + a) * GROUP], F32)
+        for h in range(1, GROUP):
+            gain = jnp.where(lane_wide >= h * PART, gain_ref[(2 * core + a) * GROUP + h], gain)
+        to_score = gain * (SCALE * LOG2E)
+        to_grad = gain * SCALE
+
+        def product(target, which, u):
+            late, part = units[u]
+            target[u] = lax.dot_general(
+                kv[a, which, key_rows(late, part)], stack(a, late, which, part), NT,
                 preferred_element_type=F32,
             )
 
-        def middle(half, quad):
-            gains = [gain_ref[(2 * core + a) * GROUP + quad * QUAD + h] for h in range(QUAD)]
-            gain = jnp.where(
-                lane_wide < 2 * HALF,
-                jnp.where(lane_wide < HALF, gains[0], gains[1]),
-                jnp.where(lane_wide < 3 * HALF, gains[2], gains[3]),
-            )
-            to_score = gain * (SCALE * LOG2E)
-            to_grad = gain * SCALE
-            lanes = pl.ds(quad * LANES, LANES)
+        def middle(u):
+            late, part = units[u]
             chunks = [pl.ds(i, CHUNK) for i in range(0, WINDOW, CHUNK)]
             top = jnp.full((8, LANES), -3e38, F32)
             for rows in chunks:
-                shade = bias[2 * x + half, rows]
-                y = s_buf[half, quad, rows] * to_score + jnp.concatenate([shade, shade], axis=1)
-                y_buf[half, quad, rows] = y
+                shade = bias[u, rows]
+                y = s_buf[u, rows] * to_score + jnp.concatenate([shade, shade], axis=1)
+                y_buf[u, rows] = y
                 top = jnp.maximum(top, jnp.max(y.reshape(CHUNK // 8, 8, LANES), axis=0))
             top = jnp.max(top, axis=0, keepdims=True)
             total = jnp.zeros((8, LANES), F32)
             dot = jnp.zeros((8, LANES), F32)
             for rows in chunks:
-                e = jnp.exp2(y_buf[half, quad, rows] - top)
-                y_buf[half, quad, rows] = e
+                e = jnp.exp2(y_buf[u, rows] - top)
+                y_buf[u, rows] = e
                 total = total + fold_rows(e)
-                dot = dot + fold_rows(e * dp_buf[half, quad, rows])
+                dot = dot + fold_rows(e * dp_buf[u, rows])
             inverse = 1.0 / jnp.sum(total, axis=0, keepdims=True)
             delta = jnp.sum(dot, axis=0, keepdims=True) * inverse
             spread = jnp.zeros((8, LANES), F32)
             for rows in chunks:
-                p = y_buf[half, quad, rows] * inverse
-                dscore = p * (dp_buf[half, quad, rows] - delta)
-                spread = spread + fold_rows(dscore * s_buf[half, quad, rows])
-                p_buf[number, half, rows, lanes] = p.astype(BF16)
-                ds_buf[number, half, rows, lanes] = (dscore * to_grad).astype(BF16)
+                p = y_buf[u, rows] * inverse
+                dscore = p * (dp_buf[u, rows] - delta)
+                spread = spread + fold_rows(dscore * s_buf[u, rows])
+                p_buf[2 * a + late, part, rows] = p.astype(BF16)
+                ds_buf[2 * a + late, part, rows] = (dscore * to_grad).astype(BF16)
             return jnp.sum(spread, axis=0, keepdims=True) * (SCALE * factor)
 
-        product(s_buf, 0, 0, 0)
-        product(s_buf, 0, 0, 1)
-        product(s_buf, 0, 1, 0)
-        product(s_buf, 0, 1, 1)
-
-        @pl.when(late == 0)
+        own = kv.at[a, :, block(2 + core)]
+        pltpu.make_async_copy(own, own, own_sem.at[a]).wait()
+        held = qg.at[a, :, pl.ds(0, BLOCK)]
+        pltpu.make_async_copy(held, held, in_sem.at[a]).wait()
+        mate_kv(a, 0).wait_recv()
+        halo_whole(a, 0).wait_recv()
+        for u in range(PARTS):
+            product(s_buf, 0, u)
+        mate_kv(a, 1).wait_recv()
+        halo_whole(a, 1).wait_recv()
+        mate_qg(a).wait_recv()
+
+        @pl.when(a == 0)
         def _():
-            mate_kv(a, 1).wait_recv()
-            halo_whole(a, 1).wait_recv()
-
-            @pl.when(a == 0)
-            def _():
-                halo_start(1)
-
-        product(dp_buf, 1, 0, 0)
-        product(dp_buf, 1, 0, 1)
-        term00 = middle(0, 0)
-        product(dp_buf, 1, 1, 0)
-        term01 = middle(0, 1)
-        product(dp_buf, 1, 1, 1)
-        term10 = middle(1, 0)
-        term11 = middle(1, 1)
-        terms = [term00 + term10, term01 + term11]
-
-        @pl.when(late == 0)
-        def _():
-            for quad in range(quads):
-                g_rows[quad] = terms[quad]
-
-        @pl.when(late == 1)
-        def _():
-            for quad in range(quads):
-                both = g_rows[quad] + terms[quad]
-                for side in range(2):
-                    index = a * (2 * quads) + quad * 2 + side
-                    g_part[pl.ds(index, 1), :] = both[:, side * 2 * HALF:(side + 1) * 2 * HALF]
-
-        return carry
-
-    lax.fori_loop(0, 4, scores, 0)
+            halo_start(1)
+
+        product(dp_buf, 1, 0)
+        terms = jnp.zeros((1, LANES), F32)
+        for u in range(len(units)):
+            if u + 1 < len(units):
+                product(dp_buf, 1, u + 1)
+            if u + PARTS < len(units):
+                product(s_buf, 0, u + PARTS)
+            terms = terms + middle(u)
+        for side in range(2):
+            g_part[pl.ds(2 * a + side, 1), :] = terms[:, side * SIDE:(side + 1) * SIDE]
+        return carry
+
+    g_part[...] = jnp.zeros(g_part.shape, F32)
+    lax.fori_loop(0, 2, scores, 0)
 
     @pl.when(me != LEADER)
     def _():
@@ -384,33 +361,30 @@
     def _():
         g_in1[LEADER] = g_part[...]
         lax.fori_loop(0, seq_size, gain_arrive, 0)
-        pairs = lax.broadcasted_iota(jnp.int32, (chips, 2 * HALF), 0)
-        lanes = lax.broadcasted_iota(jnp.int32, (chips, 2 * HALF), 1)
-        sums = jnp.zeros((chips, 2 * HALF), F32)
+        row_of = lax.broadcasted_iota(jnp.int32, (chips, SIDE), 0)
+        lanes = lax.broadcasted_iota(jnp.int32, (chips, SIDE), 1)
+        sums = jnp.zeros((chips, SIDE), F32)
         for side in range(2):
             held = g_in1[side]
             for i in range(1, chips):
                 held = held + g_in1[2 * i + side]
-            low = jnp.sum(jnp.where(lanes < HALF, held, 0.0), axis=1, keepdims=True)
-            high = jnp.sum(jnp.where(lanes < HALF, 0.0, held), axis=1, keepdims=True)
-            place = 2 * (pairs + chips * side)
-            sums = sums + jnp.where(lanes == place, low, 0.0) + jnp.where(lanes == place + 1, high, 0.0)
+            for h in range(PARTS):
+                head_sum = jnp.sum(jnp.where(lanes // PART == h, held, 0.0), axis=1, keepdims=True)
+                place = (QUERY_HEADS // 2) * side + PARTS * row_of + h
+                sums = sums + jnp.where((lanes == place) & (row_of < PARTS), head_sum, 0.0)
         g_sum[0] = jnp.sum(sums, axis=0, keepdims=True)
         pl.semaphore_wait(barrier, dp_size - 1)
         lax.fori_loop(1, dp_size, gain_send2, 0)
 
     def key_side(a, carry):
         for late in range(2):
-            x = block_of(late)
-            for half in range(2):
-                rows = key_rows(x, half)
+            for part in range(PARTS):
+                rows = key_rows(late, part)
                 acc[a, 0, rows] += jnp.dot(
-                    ds_buf[2 * a + late, half], stack(a, x, 0, half, range(GROUP)),
-                    preferred_element_type=F32,
+                    ds_buf[2 * a + late, part], stack(a, late, 0, part), preferred_element_type=F32
                 )
                 acc[a, 1, rows] += jnp.dot(
-                    p_buf[2 * a + late, half], stack(a, x, 1, half, range(GROUP)),
-                    preferred_element_type=F32,
+                    p_buf[2 * a + late, part], stack(a, late, 1, part), preferred_element_type=F32
                 )
         for place in range(2):
             for which in range(2):
@@ -425,18 +399,14 @@
 
     def query_side(a, carry):
         for late in (1, 0):
-            x = block_of(late)
-            for half in range(2):
-                turned_keys = jnp.transpose(kv[a, 0, key_rows(x, half)])
-                for quad in range(quads):
-                    ds = ds_buf[2 * a + late, half, :, pl.ds(quad * LANES, LANES)]
-                    dq = jnp.dot(turned_keys, ds, preferred_element_type=F32).astype(BF16)
-                    dq = jnp.transpose(dq)
-                    for h in range(QUAD):
-                        dq_buf[
-                            a, late, pl.ds(half * HALF, HALF),
-                            pl.ds((quad * QUAD + h) * HEAD_SIZE, HEAD_SIZE),
-                        ] = dq[h * HALF:(h + 1) * HALF]
+            for part in range(PARTS):
+                turned_keys = jnp.transpose(kv[a, 0, key_rows(late, part)])
+                dq = jnp.dot(turned_keys, ds_buf[2 * a + late, part], preferred_element_type=F32)
+                dq = jnp.transpose(dq.astype(BF16))
+                for h in range(GROUP):
+                    dq_buf[
+                        a, late, pl.ds(part * PART, PART), pl.ds(h * HEAD_SIZE, HEAD_SIZE)
+                    ] = dq[h * PART:(h + 1) * PART]
             if late:
                 dq_mate(a).start()
             else:
@@ -463,7 +433,7 @@
     def _():
         gain_copy3(mate).wait_recv()
 
-    lane1 = lax.broadcasted_iota(jnp.int32, (1, 2 * HALF), 1)
+    lane1 = lax.broadcasted_iota(jnp.int32, (1, SIDE), 1)
     for side in range(2):
         gain_out[side] = jnp.sum(jnp.where(lane1 == 2 * me + side, g_total[1], 0.0))
 
@@ -519,7 +489,6 @@
     factor = 1.0 / (dp_size * tokens * seq_size)
     hbm = pl.BlockSpec(memory_space=pltpu.HBM)
     heads = KEY_VALUE_HEADS
-    quads = GROUP // QUAD
     pair = pltpu.SemaphoreType.DMA((2,))
     four = pltpu.SemaphoreType.DMA((2, 2))
     wide = GROUP * HEAD_SIZE
@@ -544,20 +513,19 @@
             pltpu.VMEM((2, 2, BLOCK, wide), BF16),
             pltpu.VMEM((heads, 2, BLOCK, HEAD_SIZE), BF16),
             pltpu.VMEM((4 * BLOCK, BLOCK), F32),
-            pltpu.VMEM((4, WINDOW, BLOCK), F32),
-            pltpu.VMEM((2, quads, WINDOW, LANES), F32),
-            pltpu.VMEM((2, quads, WINDOW, LANES), F32),
-            pltpu.VMEM((2, quads, WINDOW, LANES), F32),
-            pltpu.VMEM((4, 2, WINDOW, quads * LANES), BF16),
-            pltpu.VMEM((4, 2, WINDOW, quads * LANES), BF16),
+            pltpu.VMEM((2 * PARTS, WINDOW, BLOCK), F32),
+            pltpu.VMEM((2 * PARTS, WINDOW, LANES), F32),
+            pltpu.VMEM((2 * PARTS, WINDOW, LANES), F32),
+            pltpu.VMEM((2 * PARTS, WINDOW, LANES), F32),
+            pltpu.VMEM((4, PARTS, WINDOW, LANES), BF16),
+            pltpu.VMEM((4, PARTS, WINDOW, LANES), BF16),
             pltpu.VMEM((1, tokens * seq_size), jnp.int32),
             pltpu.SMEM((QUERY_HEADS,), F32),
-            pltpu.VMEM((quads, 1, LANES), F32),
-            pltpu.VMEM((seq_size // 2, 2 * HALF), F32),
-            pltpu.VMEM((seq_size, seq_size // 2, 2 * HALF), F32),
-            pltpu.VMEM((1, 1, 2 * HALF), F32),
-            pltpu.VMEM((dp_size - 1, 1, 2 * HALF), F32),
-            pltpu.VMEM((2, 1, 2 * HALF), F32),
+            pltpu.VMEM((seq_size // 2, SIDE), F32),
+            pltpu.VMEM((seq_size, seq_size // 2, SIDE), F32),
+            pltpu.VMEM((1, 1, SIDE), F32),
+            pltpu.VMEM((dp_size - 1, 1, SIDE), F32),
+            pltpu.VMEM((2, 1, SIDE), F32),
             pair, pair, four, four, four, four, pair, pair,
             pair,
             pltpu.SemaphoreType.DMA((heads,)),

time: 44.1 us -> 43.7 us (level)
  no operation moved by 1% of the time
where the time goes in v5:
time: 43.7 us; the launch traced here: 43.5 us
  Pallas kernels  42.9 us (98%)
  between operations  0.64 us (1%)
    pallas_call x1, Pallas kernels, body(): pl.pallas_call(functools.partial(kernel, seq_size, dp_size, factor), out_...  40.7 us
    pallas_call x1, Pallas kernels, body(): pl.pallas_call(hand_over, out_shape=tuple((jax.ShapeDtypeStruct(x.shape,...  2.17 us

profile of v5, /device:TPU:1, one launch (start us, length us, event | category | flops | bytes accessed | tf_op | source)
XLA Modules:
  0.0 43.5 jit_solution(16114882484001787641)
XLA Ops:
  0.6 40.7 %shard_map.93 = (bf16[128,4096]{1,0:T(8,128)(2,1)}, bf16[128,512]{1,0:T(8,128)(2,1)}, bf16[128,512]{1,0:T(8,128)(2,1)}, f32[2]{0:T(128)}) custom-call(bf16[128,4096]{1,0:T(8,128)(2,1)} %bitcast.7, bf16[128,512]{1,0:T(8,128)(2,1)} %bitcast.10, bf16[128,512]{1,0:T(8,128)(2,1)} %bitcast.11, f32[32]{0:T(128)} %gain_hbm.1, bf16[128,4096]{1,0:T(8,128)(2,1)} %bitcast.8, ...), custom_call_target="tpu_custom_call" | custom-call | flops 1509949440 | bytes 4194304 | tf_op jit(solution)/shard_map/pallas_call | solution.py:495
  41.3 2.2 %shard_map.94 = (bf16[128,4096]{1,0:T(8,128)(2,1)}, bf16[128,512]{1,0:T(8,128)(2,1)}, bf16[128,512]{1,0:T(8,128)(2,1)}, f32[2]{0:T(128)}) custom-call(bf16[128,4096]{1,0:T(8,128)(2,1)} %get-tuple-element.12.dq_in, bf16[128,512]{1,0:T(8,128)(2,1)} %get-tuple-element.13.dk_in, bf16[128,512]{1,0:T(8,128)(2,1)} %get-tuple-element.14.dv_in, ...), custom_call_target="tpu_custom_call" | custom-call | tf_op jit(solution)/shard_map/pallas_call | solution.py:549

commit v6 on v5

--- a/solution.py
+++ b/solution.py
@@ -143,6 +143,9 @@
                 source.at[:, thin(head)], kv.at[a, which, block(2 + core)],
                 mate_kv_send.at[a, which], mate_kv_recv.at[a, which], mate,
             ).start()
+
+    def mate_queries_start(a):
+        head = 2 * other + a
         for which, source in enumerate((q_hbm, g_hbm)):
             remote(
                 source.at[:, wide(head)], qg.at[a, which, pl.ds(BLOCK, BLOCK)],
@@ -159,6 +162,8 @@
 
     halo_start(0)
     mate_start(0)
+    mate_queries_start(0)
+    halo_start(1)
     mate_start(1)
     acc[...] = jnp.zeros(acc.shape, F32)
     seg_copy.wait()
@@ -260,9 +265,7 @@
             [qg[a, which, rows, pl.ds(h * HEAD_SIZE, HEAD_SIZE)] for h in range(GROUP)], axis=0
         )
 
-    units = [(late, part) for late in range(2) for part in range(PARTS)]
-
-    def scores(a, carry):
+    def scores(late, a):
         gain = jnp.full((1, LANES), gain_ref[(2 * core + a) * GROUP], F32)
         for h in range(1, GROUP):
             gain = jnp.where(lane_wide >= h * PART, gain_ref[(2 * core + a) * GROUP + h], gain)
@@ -270,18 +273,16 @@
         to_grad = gain * SCALE
 
         def product(target, which, u):
-            late, part = units[u]
             target[u] = lax.dot_general(
-                kv[a, which, key_rows(late, part)], stack(a, late, which, part), NT,
+                kv[a, which, key_rows(late, u)], stack(a, late, which, u), NT,
                 preferred_element_type=F32,
             )
 
         def middle(u):
-            late, part = units[u]
             chunks = [pl.ds(i, CHUNK) for i in range(0, WINDOW, CHUNK)]
             top = jnp.full((8, LANES), -3e38, F32)
             for rows in chunks:
-                shade = bias[u, rows]
+                shade = bias[late * PARTS + u, rows]
                 y = s_buf[u, rows] * to_score + jnp.concatenate([shade, shade], axis=1)
                 y_buf[u, rows] = y
                 top = jnp.maximum(top, jnp.max(y.reshape(CHUNK // 8, 8, LANES), axis=0))
@@ -300,40 +301,49 @@
                 p = y_buf[u, rows] * inverse
                 dscore = p * (dp_buf[u, rows] - delta)
                 spread = spread + fold_rows(dscore * s_buf[u, rows])
-                p_buf[2 * a + late, part, rows] = p.astype(BF16)
-                ds_buf[2 * a + late, part, rows] = (dscore * to_grad).astype(BF16)
+                p_buf[2 * a + late, u, rows] = p.astype(BF16)
+                ds_buf[2 * a + late, u, rows] = (dscore * to_grad).astype(BF16)
             return jnp.sum(spread, axis=0, keepdims=True) * (SCALE * factor)
 
-        own = kv.at[a, :, block(2 + core)]
-        pltpu.make_async_copy(own, own, own_sem.at[a]).wait()
-        held = qg.at[a, :, pl.ds(0, BLOCK)]
-        pltpu.make_async_copy(held, held, in_sem.at[a]).wait()
-        mate_kv(a, 0).wait_recv()
-        halo_whole(a, 0).wait_recv()
+        if late:
+            mate_qg(a).wait_recv()
+        else:
+            own = kv.at[a, :, block(2 + core)]
+            pltpu.make_async_copy(own, own, own_sem.at[a]).wait()
+            held = qg.at[a, :, pl.ds(0, BLOCK)]
+            pltpu.make_async_copy(held, held, in_sem.at[a]).wait()
+            mate_kv(a, 0).wait_recv()
+            halo_whole(a, 0).wait_recv()
         for u in range(PARTS):
             product(s_buf, 0, u)
-        mate_kv(a, 1).wait_recv()
-        halo_whole(a, 1).wait_recv()
-        mate_qg(a).wait_recv()
+        if not late:
+            mate_kv(a, 1).wait_recv()
+            halo_whole(a, 1).wait_recv()
+        product(dp_buf, 1, 0)
+        terms = jnp.zeros((1, LANES), F32)
+        for u in range(PARTS):
+            if u + 1 < PARTS:
+                product(dp_buf, 1, u + 1)
+            terms = terms + middle(u)
+        for side in range(2):
+            g_part[pl.ds(2 * a + side, 1), :] += terms[:, side * SIDE:(side + 1) * SIDE]
+
+    def own_scores(a, carry):
+        scores(0, a)
 
         @pl.when(a == 0)
         def _():
-            halo_start(1)
-
-        product(dp_buf, 1, 0)
-        terms = jnp.zeros((1, LANES), F32)
-        for u in range(len(units)):
-            if u + 1 < len(units):
-                product(dp_buf, 1, u + 1)
-            if u + PARTS < len(units):
-                product(s_buf, 0, u + PARTS)
-            terms = terms + middle(u)
-        for side in range(2):
-            g_part[pl.ds(2 * a + side, 1), :] = terms[:, side * SIDE:(side + 1) * SIDE]
+            mate_queries_start(1)
+
+        return carry
+
+    def mate_scores(a, carry):
+        scores(1, a)
         return carry
 
     g_part[...] = jnp.zeros(g_part.shape, F32)
-    lax.fori_loop(0, 2, scores, 0)
+    lax.fori_loop(0, 2, own_scores, 0)
+    lax.fori_loop(0, 2, mate_scores, 0)
 
     @pl.when(me != LEADER)
     def _():
@@ -514,9 +524,9 @@
             pltpu.VMEM((heads, 2, BLOCK, HEAD_SIZE), BF16),
             pltpu.VMEM((4 * BLOCK, BLOCK), F32),
             pltpu.VMEM((2 * PARTS, WINDOW, BLOCK), F32),
-            pltpu.VMEM((2 * PARTS, WINDOW, LANES), F32),
-            pltpu.VMEM((2 * PARTS, WINDOW, LANES), F32),
-            pltpu.VMEM((2 * PARTS, WINDOW, LANES), F32),
+            pltpu.VMEM((PARTS, WINDOW, LANES), F32),
+            pltpu.VMEM((PARTS, WINDOW, LANES), F32),
+            pltpu.VMEM((PARTS, WINDOW, LANES), F32),
             pltpu.VMEM((4, PARTS, WINDOW, LANES), BF16),
             pltpu.VMEM((4, PARTS, WINDOW, LANES), BF16),
             pltpu.VMEM((1, tokens * seq_size), jnp.int32),

time: 43.7 us -> 42.3 us (0.968)
  Pallas kernels: 42.9 us -> 41.5 us
    pallas_call x1, Pallas kernels: 40.7 us -> 39.4 us  [body(): pl.pallas_call(functools.partial(kernel, seq_size, dp_size, factor), out_...]
where the time goes in v6:
time: 42.3 us; the launch traced here: 42.2 us
  Pallas kernels  41.5 us (98%)
  between operations  0.64 us (2%)
    pallas_call x1, Pallas kernels, body(): pl.pallas_call(functools.partial(kernel, seq_size, dp_size, factor), out_...  39.4 us
    pallas_call x1, Pallas kernels, body(): pl.pallas_call(hand_over, out_shape=tuple((jax.ShapeDtypeStruct(x.shape,...  2.17 us

profile of v6, /device:TPU:1, one launch (start us, length us, event | category | flops | bytes accessed | tf_op | source)
XLA Modules:
  0.0 42.2 jit_solution(8642880257622004552)
XLA Ops:
  0.6 39.4 %shard_map.93 = (bf16[128,4096]{1,0:T(8,128)(2,1)}, bf16[128,512]{1,0:T(8,128)(2,1)}, bf16[128,512]{1,0:T(8,128)(2,1)}, f32[2]{0:T(128)}) custom-call(bf16[128,4096]{1,0:T(8,128)(2,1)} %bitcast.7, bf16[128,512]{1,0:T(8,128)(2,1)} %bitcast.10, bf16[128,512]{1,0:T(8,128)(2,1)} %bitcast.11, f32[32]{0:T(128)} %gain_hbm.1, bf16[128,4096]{1,0:T(8,128)(2,1)} %bitcast.8, ...), custom_call_target="tpu_custom_call" | custom-call | flops 1509949440 | bytes 4194304 | tf_op jit(solution)/shard_map/pallas_call | solution.py:505
  40.0 2.2 %shard_map.94 = (bf16[128,4096]{1,0:T(8,128)(2,1)}, bf16[128,512]{1,0:T(8,128)(2,1)}, bf16[128,512]{1,0:T(8,128)(2,1)}, f32[2]{0:T(128)}) custom-call(bf16[128,4096]{1,0:T(8,128)(2,1)} %get-tuple-element.12.dq_in, bf16[128,512]{1,0:T(8,128)(2,1)} %get-tuple-element.13.dk_in, bf16[128,512]{1,0:T(8,128)(2,1)} %get-tuple-element.14.dv_in, ...), custom_call_target="tpu_custom_call" | custom-call | tf_op jit(solution)/shard_map/pallas_call | solution.py:559

commit v7 on v6

--- a/solution.py
+++ b/solution.py
@@ -19,7 +19,7 @@
 LANES = GROUP * PART
 SIDE = 128
 CHUNK = 32
-HAND_PARTS = 4
+HAND_PARTS = 8
 LEADER = 7
 VMEM_BYTES = 64 * 1024 * 1024
 LOG2E = math.log2(math.e)
@@ -319,6 +319,11 @@
         if not late:
             mate_kv(a, 1).wait_recv()
             halo_whole(a, 1).wait_recv()
+
+            @pl.when(a == 0)
+            def _():
+                mate_queries_start(1)
+
         product(dp_buf, 1, 0)
         terms = jnp.zeros((1, LANES), F32)
         for u in range(PARTS):
@@ -330,11 +335,6 @@
 
     def own_scores(a, carry):
         scores(0, a)
-
-        @pl.when(a == 0)
-        def _():
-            mate_queries_start(1)
-
         return carry
 
     def mate_scores(a, carry):
@@ -356,15 +356,20 @@
 
         return carry
 
-    def gain_send2(i, carry):
-        pltpu.make_async_remote_copy(
-            src_ref=g_sum.at[0],
-            dst_ref=g_in2.at[i - 1],
-            send_sem=gain2_sem.at[0],
-            recv_sem=gain2_sem.at[1],
-            device_id={"dp": lax.rem(row + i, dp_size)},
-            device_id_type=pl.DeviceIdType.MESH,
-        ).start()
+    def gain_send2(target, carry):
+        offset = lax.rem(target - row + dp_size, dp_size)
+
+        @pl.when(offset != 0)
+        def _():
+            pltpu.make_async_remote_copy(
+                src_ref=g_sum.at[0],
+                dst_ref=g_in2.at[offset - 1],
+                send_sem=gain2_sem.at[0],
+                recv_sem=gain2_sem.at[1],
+                device_id={"dp": target},
+                device_id_type=pl.DeviceIdType.MESH,
+            ).start()
+
         return carry
 
     @pl.when(me == LEADER)
@@ -384,7 +389,7 @@
                 sums = sums + jnp.where((lanes == place) & (row_of < PARTS), head_sum, 0.0)
         g_sum[0] = jnp.sum(sums, axis=0, keepdims=True)
         pl.semaphore_wait(barrier, dp_size - 1)
-        lax.fori_loop(1, dp_size, gain_send2, 0)
+        lax.fori_loop(0, dp_size, gain_send2, 0)
 
     def key_side(a, carry):
         for late in range(2):
@@ -428,15 +433,18 @@
     finish(1)
     gain2_whole = remote(g_in2, g_in2, gain2_sem.at[0], gain2_sem.at[1], mate)
 
-    def gain_send3(i, carry):
-        gain_copy3(lax.rem(me + i, seq_size)).start()
+    def gain_send3(target, carry):
+        @pl.when(target != LEADER)
+        def _():
+            gain_copy3(target).start()
+
         return carry
 
     @pl.when(me == LEADER)
     def _():
         gain2_whole.wait_recv()
         g_total[0] = g_sum[0] + jnp.sum(g_in2[...], axis=0)
-        lax.fori_loop(1, seq_size, gain_send3, 0)
+        lax.fori_loop(0, seq_size, gain_send3, 0)
         g_total[1] = g_total[0]
 
     @pl.when(me != LEADER)

time: 42.3 us -> 42 us (level)
  no operation moved by 1% of the time
where the time goes in v7:
time: 42 us; the launch traced here: 41.9 us
  Pallas kernels  41.2 us (98%)
  between operations  0.64 us (2%)
    pallas_call x1, Pallas kernels, body(): pl.pallas_call(functools.partial(kernel, seq_size, dp_size, factor), out_...  39 us
    pallas_call x1, Pallas kernels, body(): pl.pallas_call(hand_over, out_shape=tuple((jax.ShapeDtypeStruct(x.shape,...  2.23 us

profile of v7, /device:TPU:1, one launch (start us, length us, event | category | flops | bytes accessed | tf_op | source)
XLA Modules:
  0.0 41.9 jit_solution(9129454717671872711)
XLA Ops:
  0.6 39.0 %shard_map.93 = (bf16[128,4096]{1,0:T(8,128)(2,1)}, bf16[128,512]{1,0:T(8,128)(2,1)}, bf16[128,512]{1,0:T(8,128)(2,1)}, f32[2]{0:T(128)}) custom-call(bf16[128,4096]{1,0:T(8,128)(2,1)} %bitcast.7, bf16[128,512]{1,0:T(8,128)(2,1)} %bitcast.10, bf16[128,512]{1,0:T(8,128)(2,1)} %bitcast.11, f32[32]{0:T(128)} %gain_hbm.1, bf16[128,4096]{1,0:T(8,128)(2,1)} %bitcast.8, ...), custom_call_target="tpu_custom_call" | custom-call | flops 1509949440 | bytes 4194304 | tf_op jit(solution)/shard_map/pallas_call | solution.py:513
  39.6 2.2 %shard_map.94 = (bf16[128,4096]{1,0:T(8,128)(2,1)}, bf16[128,512]{1,0:T(8,128)(2,1)}, bf16[128,512]{1,0:T(8,128)(2,1)}, f32[2]{0:T(128)}) custom-call(bf16[128,4096]{1,0:T(8,128)(2,1)} %get-tuple-element.12.dq_in, bf16[128,512]{1,0:T(8,128)(2,1)} %get-tuple-element.13.dk_in, bf16[128,512]{1,0:T(8,128)(2,1)} %get-tuple-element.14.dv_in, ...), custom_call_target="tpu_custom_call" | custom-call | tf_op jit(solution)/shard_map/pallas_call | solution.py:567

commit v8 on v7

--- a/solution.py
+++ b/solution.py
@@ -163,7 +163,6 @@
     halo_start(0)
     mate_start(0)
     mate_queries_start(0)
-    halo_start(1)
     mate_start(1)
     acc[...] = jnp.zeros(acc.shape, F32)
     seg_copy.wait()
@@ -314,6 +313,11 @@
             pltpu.make_async_copy(held, held, in_sem.at[a]).wait()
             mate_kv(a, 0).wait_recv()
             halo_whole(a, 0).wait_recv()
+
+            @pl.when(a == 0)
+            def _():
+                halo_start(1)
+
         for u in range(PARTS):
             product(s_buf, 0, u)
         if not late:

time: 42 us -> 42.9 us (1.021)
  Pallas kernels: 41.2 us -> 42.1 us
    pallas_call x1, Pallas kernels: 39 us -> 39.9 us  [body(): pl.pallas_call(functools.partial(kernel, seq_size, dp_size, factor), out_...]
where the time goes in v8:
time: 42.9 us; the launch traced here: 42.8 us
  Pallas kernels  42.1 us (98%)
  between operations  0.64 us (1%)
    pallas_call x1, Pallas kernels, body(): pl.pallas_call(functools.partial(kernel, seq_size, dp_size, factor), out_...  39.9 us
    pallas_call x1, Pallas kernels, body(): pl.pallas_call(hand_over, out_shape=tuple((jax.ShapeDtypeStruct(x.shape,...  2.23 us

profile of v8, /device:TPU:1, one launch (start us, length us, event | category | flops | bytes accessed | tf_op | source)
XLA Modules:
  0.0 42.8 jit_solution(7863828124501327723)
XLA Ops:
  0.6 39.9 %shard_map.93 = (bf16[128,4096]{1,0:T(8,128)(2,1)}, bf16[128,512]{1,0:T(8,128)(2,1)}, bf16[128,512]{1,0:T(8,128)(2,1)}, f32[2]{0:T(128)}) custom-call(bf16[128,4096]{1,0:T(8,128)(2,1)} %bitcast.7, bf16[128,512]{1,0:T(8,128)(2,1)} %bitcast.10, bf16[128,512]{1,0:T(8,128)(2,1)} %bitcast.11, f32[32]{0:T(128)} %gain_hbm.1, bf16[128,4096]{1,0:T(8,128)(2,1)} %bitcast.8, ...), custom_call_target="tpu_custom_call" | custom-call | flops 1509949440 | bytes 4194304 | tf_op jit(solution)/shard_map/pallas_call | solution.py:517
  40.5 2.2 %shard_map.94 = (bf16[128,4096]{1,0:T(8,128)(2,1)}, bf16[128,512]{1,0:T(8,128)(2,1)}, bf16[128,512]{1,0:T(8,128)(2,1)}, f32[2]{0:T(128)}) custom-call(bf16[128,4096]{1,0:T(8,128)(2,1)} %get-tuple-element.12.dq_in, bf16[128,512]{1,0:T(8,128)(2,1)} %get-tuple-element.13.dk_in, bf16[128,512]{1,0:T(8,128)(2,1)} %get-tuple-element.14.dv_in, ...), custom_call_target="tpu_custom_call" | custom-call | tf_op jit(solution)/shard_map/pallas_call | solution.py:571
